TPU v7x, 32 devices: a whole 2x2x4 slice. The times are simulated.
32 devices in a mesh: grp: 2 (over y), ew: 4 (over z), ns: 2 (over x), lvl: 2 (over core).
Axes of the slice: x: 2, y: 2, z: 4, core: 2. Of those that a mesh axis runs over, the one named last changes fastest.
Arguments:
- probe_fine: int32 [8, 128, 512], P('lvl', 'ew', 'ns'), may hold values from 0 to 1
- probe_coarse: int32 [8, 64, 256], P('lvl', 'ew', 'ns'), may hold values from 0 to 1
- kappa_fine: float32 [256, 512], P(('grp', 'ew'), 'ns'), parts along dimension 0, may hold values from 0.2 to 2
- kappa_coarse: float32 [128, 256], P(('grp', 'ew'), 'ns'), parts along dimension 0, may hold values from 0.2 to 2
- phi_tiles: float32 [1024, 128, 128], P(('ew', 'ns')), may hold values from -0.5 to 0.5
- obs_weight: float32 [2048, 128], P(('grp', 'ew', 'ns')), parts along dimension 0, may hold values from 4 to 40
- block_index: int32 [1024], P(('ew', 'ns')), may hold values from 0 to 85, as said below
- block_count: int32 [8], P(('ew', 'ns')), may hold values from 2 to 128, as said below
Outputs:
- solve_fine: float32 [16, 128, 512], P(('grp', 'lvl'), 'ew', 'ns'), parts along dimension 0
- solve_coarse: float32 [16, 64, 256], P(('grp', 'lvl'), 'ew', 'ns'), parts along dimension 0
- resid_fine: float32 [16, 128, 512], P(('grp', 'lvl'), 'ew', 'ns'), parts along dimension 0
- resid_coarse: float32 [16, 64, 256], P(('grp', 'lvl'), 'ew', 'ns'), parts along dimension 0
There are 2 independent parts, one for each index of `grp`. A program takes and returns all parts, laid end to end along the dimension named above; an argument that names none is the same for every part. Nothing has to cross between parts.
Inputs may be any that keep to these rules, and one draw needn't show every extreme that they name: `block_count`: every device has 2 or more live blocks, and only blocks below its count carry observations; some device has all 128 slots live. `block_index`: A block's tile is one of its own device's 86 tiles, in the order of the tile list; each device's first block names a tile of its western outside row (fine or coarse) and its second block a tile of its eastern outside row.
All inputs are finite; a program needn't handle non-finite values.
Results may differ from a plain program's by a relative error of at most 0.0003.
Values sent between devices are 32-bit elements; how exact they have to be, the bound alone decides.
A program may use at most 64 MiB of HBM per device.

v0:
```python
import jax
import jax.numpy as jnp
from jax import lax
from jax.sharding import PartitionSpec as P

ITERS = 2


def with_halo(block, sides, width):
    for axis, dim in sides:
        count = lax.axis_size(axis)
        forward = [(i, i + 1) for i in range(count - 1)]
        backward = [(target, source) for source, target in forward]
        low = lax.ppermute(
            lax.slice_in_dim(block, block.shape[dim] - width, None, axis=dim), axis, forward
        )
        high = lax.ppermute(lax.slice_in_dim(block, 0, width, axis=dim), axis, backward)
        block = jnp.concatenate([low, block, high], axis=dim)
    return block


def shifted(block, axis, distance):
    devices = range(lax.axis_size(axis))
    route = [(i - distance, i) for i in devices if i - distance in devices]
    return lax.ppermute(block, axis, route)


def apply_sar(padded, kappa):
    centre = padded[:, 1:-1, 1:-1]
    beside_all = (
        padded[:, 2:, 1:-1] + padded[:, :-2, 1:-1] + padded[:, 1:-1, 2:] + padded[:, 1:-1, :-2]
    )
    return (4.0 + kappa) * centre - beside_all


def fine_faces(field):
    return with_halo(field, (("ew", 1), ("ns", 2)), 1)


def coarse_faces(field):
    return with_halo(field, (("ew", 1), ("ns", 2)), 1)


def local_products(first_fine, first_coarse, second_fine, second_coarse):
    return jnp.sum(first_fine * second_fine, axis=(1, 2)) + jnp.sum(
        first_coarse * second_coarse, axis=(1, 2)
    )


def local(
    probe_fine,
    probe_coarse,
    kappa_fine,
    kappa_coarse,
    phi_tiles,
    obs_weight,
    block_index,
    block_count,
):
    probes, rows, width = probe_fine.shape
    half_rows = probe_coarse.shape[1]
    tile = phi_tiles.shape[1]
    blocks = phi_tiles.shape[0]
    fine_count = (rows + 2) * (width // tile)
    tile_total = fine_count + half_rows + 2
    live = (jnp.arange(blocks, dtype=jnp.int32) < block_count[0]).astype(jnp.float32)
    weights = (obs_weight * live[:, None])[None]
    onehot = (block_index[:, None] == jnp.arange(tile_total, dtype=jnp.int32)[None, :]).astype(
        jnp.float32
    )
    resid_fine = (2 * probe_fine - 1).astype(jnp.float32)
    resid_coarse = (2 * probe_coarse - 1).astype(jnp.float32)
    solve_fine = jnp.zeros_like(resid_fine)
    solve_coarse = jnp.zeros_like(resid_coarse)

    def squares(first_fine, first_coarse):
        return lax.psum(
            local_products(first_fine, first_coarse, first_fine, first_coarse), ("ew", "ns")
        )

    direction_fine, direction_coarse = (resid_fine, resid_coarse)
    norm_now = squares(resid_fine, resid_coarse)
    for iteration in range(ITERS):
        halo_fine = fine_faces(direction_fine)
        halo_coarse = coarse_faces(direction_coarse)
        prior_fine = apply_sar(fine_faces(apply_sar(halo_fine, kappa_fine)), kappa_fine)
        prior_coarse = apply_sar(coarse_faces(apply_sar(halo_coarse, kappa_coarse)), kappa_coarse)
        rows_fine = halo_fine[:, :, 1:-1]
        rows_coarse = halo_coarse[:, :, 1:-1]
        ext = jnp.concatenate([rows_fine.reshape(probes, fine_count, tile), rows_coarse], axis=1)
        picked = jnp.take(ext, block_index, axis=1)
        seen = jnp.einsum(
            "bij,pbj->pbi",
            phi_tiles,
            picked,
            precision=lax.Precision.HIGHEST,
            preferred_element_type=jnp.float32,
        )
        scaled = seen * weights
        back = jnp.einsum(
            "bij,pbi->pbj",
            phi_tiles,
            scaled,
            precision=lax.Precision.HIGHEST,
            preferred_element_type=jnp.float32,
        )
        adjoint = jnp.einsum("pbj,bt->ptj", back, onehot, precision=lax.Precision.HIGHEST)
        adj_fine = adjoint[:, :fine_count].reshape(probes, rows + 2, width)
        adj_coarse = adjoint[:, fine_count:]
        west_row = jnp.concatenate([adj_fine[:, 0], adj_coarse[:, 0]], axis=-1)
        east_row = jnp.concatenate([adj_fine[:, -1], adj_coarse[:, -1]], axis=-1)
        from_next = shifted(west_row, "ew", -1)
        from_prev = shifted(east_row, "ew", 1)
        inner_fine = adj_fine[:, 1:-1]
        inner_fine = (
            inner_fine.at[:, 0].add(from_prev[:, :width]).at[:, -1].add(from_next[:, :width])
        )
        inner_coarse = adj_coarse[:, 1:-1]
        inner_coarse = (
            inner_coarse.at[:, 0].add(from_prev[:, width:]).at[:, -1].add(from_next[:, width:])
        )
        image_fine = prior_fine + inner_fine
        image_coarse = prior_coarse + inner_coarse
        curve = lax.psum(
            local_products(direction_fine, direction_coarse, image_fine, image_coarse), ("ew", "ns")
        )
        alpha = (norm_now / curve)[:, None, None]
        solve_fine = solve_fine + alpha * direction_fine
        solve_coarse = solve_coarse + alpha * direction_coarse
        resid_fine = resid_fine - alpha * image_fine
        resid_coarse = resid_coarse - alpha * image_coarse
        if iteration + 1 < ITERS:
            norm_next = squares(resid_fine, resid_coarse)
            ratio = (norm_next / norm_now)[:, None, None]
            direction_fine = resid_fine + ratio * direction_fine
            direction_coarse = resid_coarse + ratio * direction_coarse
            norm_now = norm_next
    return (solve_fine, solve_coarse, resid_fine, resid_coarse)


def solution(mesh):
    in_specs = (
        P("lvl", "ew", "ns"),
        P("lvl", "ew", "ns"),
        P(("grp", "ew"), "ns"),
        P(("grp", "ew"), "ns"),
        P(("ew", "ns"), None, None),
        P(("grp", "ew", "ns"), None),
        P(("ew", "ns")),
        P(("ew", "ns")),
    )
    out_specs = (
        P(("grp", "lvl"), "ew", "ns"),
        P(("grp", "lvl"), "ew", "ns"),
        P(("grp", "lvl"), "ew", "ns"),
        P(("grp", "lvl"), "ew", "ns"),
    )
    return jax.shard_map(local, mesh=mesh, in_specs=in_specs, out_specs=out_specs, check_vma=False)
```

profile of v0, /device:TPU:0, one launch (start us, length us, event | category | flops | bytes accessed | tf_op | source)
XLA Modules:
  0.0 239.9 jit_solution(14725809653699780462)
XLA Ops:
  1.4 1.3 collective-permute-start.9
  2.7 5.6 %collective-permute-start.8 = (f32[4,1,128]{2,1,0:T(1,128)S(1)}, f32[4,1,128]{2,1,0:T(1,128)S(1)}, u32[]{:S(2)}, u32[]{:S(2)}) collective-permute-start(f32[4,1,128]{2,1,0:T(1,128)S(1)} %get-tuple-element.164), channel_id=1, source_target_pairs={{0,4},{4,8},{8,12},{1,5},{5,9},{9,13},{2,6},{6,10},{10,14},{3,7},{... | collective-permute-start | bytes 6152 | tf_op jit(solution)/shard_map/ppermute | solution.py:14
  9.3 1.3 collective-permute-start
  10.6 4.6 %collective-permute-start.1 = (f32[4,1,256]{2,0,1:T(4,128)S(1)}, f32[4,1,256]{2,0,1:T(4,128)S(1)}, u32[]{:S(2)}, u32[]{:S(2)}) collective-permute-start(f32[4,1,256]{2,0,1:T(4,128)S(1)} %get-tuple-element.146), channel_id=1, source_target_pairs={{0,4},{4,8},{8,12},{1,5},{5,9},{9,13},{2,6},{6,10},{10,14},{3,7},{... | collective-permute-start | bytes 12296 | tf_op jit(solution)/shard_map/ppermute | solution.py:14
  19.6 3.8 %collective-permute-start.13 = (f32[4,18,1]{2,1,0:T(8,128)S(1)}, f32[4,18,1]{2,1,0:T(8,128)S(1)}, u32[]{:S(2)}, u32[]{:S(2)}) collective-permute-start(f32[4,18,1]{2,1,0:T(8,128)S(1)} %get-tuple-element.155), channel_id=1, source_target_pairs={{0,2},{1,3},{4,6},{5,7},{8,10},{9,11},{12,14},{13,15},{16,18},{17,... | collective-permute-start | bytes 872 | tf_op jit(solution)/shard_map/ppermute | solution.py:14
  23.5 1.3 collective-permute-start.12
  25.2 4.3 %collective-permute-done.12 = f32[4,18,1]{2,1,0:T(8,128)S(1)} collective-permute-done((f32[4,18,1]{2,1,0:T(8,128)S(1)}, f32[4,18,1]{2,1,0:T(8,128)S(1)}, u32[]{:S(2)}, u32[]{:S(2)}) %collective-permute-start.12) | collective-permute-done | bytes 320 | tf_op jit(solution)/shard_map/ppermute | solution.py:17
  29.6 1.3 collective-permute-start.14
  30.9 4.5 %collective-permute-start.15 = (f32[4,1,128]{2,1,0:T(1,128)S(1)}, f32[4,1,128]{2,1,0:T(1,128)S(1)}, u32[]{:S(2)}, u32[]{:S(2)}) collective-permute-start(f32[4,1,128]{2,1,0:T(1,128)S(1)} %get-tuple-element.162), channel_id=1, source_target_pairs={{0,4},{4,8},{8,12},{1,5},{5,9},{9,13},{2,6},{6,10},{10,14},{3,7},{... | collective-permute-start | bytes 6152 | tf_op jit(solution)/shard_map/ppermute | solution.py:14
  36.3 16.4 %fusion.1 = f32[4,128,128]{2,0,1:T(4,128)S(1)} fusion(f32[128,128,128]{2,1,0:T(8,128)} %param.30, f32[128,4,128]{2,1,0:T(4,128)S(1)} %gather_fusion, f32[128,128]{1,0:T(8,128)S(1)} %broadcast_multiply_fusion, pred[128]{0:T(512)(128)(4,1)S(1)} %compare_and_fusion), kind=kOutput, calls=%fused_computation.5 | convolution fusion | flops 100794368 | bytes 8978560 | tf_op jit(solution)/shard_map/bij,pbj->pbi/dot_general | solution.py:92
  52.7 7.3 %fusion.92 = f32[128,4,128]{2,1,0:T(4,128)S(1)} fusion(f32[4,128,128]{2,0,1:T(4,128)S(1)} %fusion.1, f32[128,128,128]{2,1,0:T(8,128)S(1)} %copy-done), kind=kOutput, calls=%fused_computation.209 | convolution fusion | flops 100663296 | bytes 8912896 | tf_op jit(solution)/shard_map/bij,pbi->pbj/dot_general | solution.py:100
  60.6 3.5 %collective-permute-start.10 = (f32[4,384]{1,0:T(4,128)S(1)}, f32[4,384]{1,0:T(4,128)S(1)}, u32[]{:S(2)}, u32[]{:S(2)}) collective-permute-start(f32[4,384]{1,0:T(4,128)S(1)} %pad_maximum_fusion.74), channel_id=1, source_target_pairs={{0,4},{4,8},{8,12},{1,5},{5,9},{9,13},{2,6},{6,10},{10,14},{3,7},{... | collective-permute-start | bytes 18440 | tf_op jit(solution)/shard_map/ppermute | solution.py:25
  64.1 1.6 collective-permute-start.3
  65.7 1.5 collective-permute-start.2
  67.6 4.5 %collective-permute-done.2 = f32[4,34,1]{2,0,1:T(4,128)S(1)} collective-permute-done((f32[4,34,1]{2,0,1:T(4,128)S(1)}, f32[4,34,1]{2,0,1:T(4,128)S(1)}, u32[]{:S(2)}, u32[]{:S(2)}) %collective-permute-start.2) | collective-permute-done | bytes 576 | tf_op jit(solution)/shard_map/ppermute | solution.py:17
  72.4 1.3 collective-permute-start.4
  73.7 4.5 %collective-permute-start.5 = (f32[4,1,256]{2,0,1:T(4,128)S(1)}, f32[4,1,256]{2,0,1:T(4,128)S(1)}, u32[]{:S(2)}, u32[]{:S(2)}) collective-permute-start(f32[4,1,256]{2,0,1:T(4,128)S(1)} %get-tuple-element.144), channel_id=1, source_target_pairs={{0,4},{4,8},{8,12},{1,5},{5,9},{9,13},{2,6},{6,10},{10,14},{3,7},{... | collective-permute-start | bytes 12296 | tf_op jit(solution)/shard_map/ppermute | solution.py:14
  78.3 1.6 collective-permute-start.17
  79.9 1.3 collective-permute-start.16
  81.3 4.5 %collective-permute-start.7 = (f32[4,34,1]{2,0,1:T(4,128)S(1)}, f32[4,34,1]{2,0,1:T(4,128)S(1)}, u32[]{:S(2)}, u32[]{:S(2)}) collective-permute-start(f32[4,34,1]{2,0,1:T(4,128)S(1)} %get-tuple-element.135), channel_id=1, source_target_pairs={{0,2},{1,3},{4,6},{5,7},{8,10},{9,11},{12,14},{13,15},{16,18},{17,... | collective-permute-start | bytes 1640 | tf_op jit(solution)/shard_map/ppermute | solution.py:14
  85.9 1.3 collective-permute-start.6
  87.2 1.3 collective-permute-start.11
  88.6 4.2 %collective-permute-done.11 = f32[4,384]{1,0:T(4,128)S(1)} collective-permute-done((f32[4,384]{1,0:T(4,128)S(1)}, f32[4,384]{1,0:T(4,128)S(1)}, u32[]{:S(2)}, u32[]{:S(2)}) %collective-permute-start.11) | collective-permute-done | bytes 6176 | tf_op jit(solution)/shard_map/ppermute | solution.py:25
  93.5 19.8 %all-reduce = (f32[4]{0:T(128)S(1)}, f32[4]{0:T(128)S(1)}) all-reduce(f32[4]{0:T(128)S(1)} %add.192, f32[4]{0:T(128)S(1)} %add.213), channel_id=1, replica_groups=mesh['grp'=2,'ew'=4,'ns'=2,'lvl'=2] {'ew','ns'}, use_global_device_ids=true, to_apply=%region_2.0 | all-reduce | flops 8 | bytes 64 | tf_op jit(solution)/shard_map/psum | solution.py:77
  113.7 17.2 %psum.30 = f32[4]{0:T(128)S(1)} all-reduce(f32[4]{0:T(128)S(1)} %add.214), channel_id=1, replica_groups=mesh['grp'=2,'ew'=4,'ns'=2,'lvl'=2] {'ew','ns'}, use_global_device_ids=true, to_apply=%region_8.10 | all-reduce | flops 4 | bytes 32 | tf_op jit(solution)/shard_map/psum | solution.py:77
  131.2 1.3 collective-permute-start.27
  132.5 4.5 %collective-permute-start.26 = (f32[4,1,128]{2,1,0:T(1,128)S(1)}, f32[4,1,128]{2,1,0:T(1,128)S(1)}, u32[]{:S(2)}, u32[]{:S(2)}) collective-permute-start(f32[4,1,128]{2,1,0:T(1,128)S(1)} %get-tuple-element.160), channel_id=1, source_target_pairs={{0,4},{4,8},{8,12},{1,5},{5,9},{9,13},{2,6},{6,10},{10,14},{3,7},{... | collective-permute-start | bytes 6152 | tf_op jit(solution)/shard_map/ppermute | solution.py:14
  138.4 3.8 %collective-permute-start.31 = (f32[4,18,1]{2,1,0:T(8,128)S(1)}, f32[4,18,1]{2,1,0:T(8,128)S(1)}, u32[]{:S(2)}, u32[]{:S(2)}) collective-permute-start(f32[4,18,1]{2,1,0:T(8,128)S(1)} %get-tuple-element.151), channel_id=1, source_target_pairs={{0,2},{1,3},{4,6},{5,7},{8,10},{9,11},{12,14},{13,15},{16,18},{17,... | collective-permute-start | bytes 872 | tf_op jit(solution)/shard_map/ppermute | solution.py:14
  142.2 1.3 collective-permute-start.30
  143.5 1.3 collective-permute-start.18
  144.8 4.8 %collective-permute-start.19 = (f32[4,1,256]{2,0,1:T(4,128)S(1)}, f32[4,1,256]{2,0,1:T(4,128)S(1)}, u32[]{:S(2)}, u32[]{:S(2)}) collective-permute-start(f32[4,1,256]{2,0,1:T(4,128)S(1)} %get-tuple-element.142), channel_id=1, source_target_pairs={{0,4},{4,8},{8,12},{1,5},{5,9},{9,13},{2,6},{6,10},{10,14},{3,7},{... | collective-permute-start | bytes 12296 | tf_op jit(solution)/shard_map/ppermute | solution.py:14
  149.8 1.3 collective-permute-start.32
  151.1 4.6 %collective-permute-start.33 = (f32[4,1,128]{2,1,0:T(1,128)S(1)}, f32[4,1,128]{2,1,0:T(1,128)S(1)}, u32[]{:S(2)}, u32[]{:S(2)}) collective-permute-start(f32[4,1,128]{2,1,0:T(1,128)S(1)} %get-tuple-element.158), channel_id=1, source_target_pairs={{0,4},{4,8},{8,12},{1,5},{5,9},{9,13},{2,6},{6,10},{10,14},{3,7},{... | collective-permute-start | bytes 6152 | tf_op jit(solution)/shard_map/ppermute | solution.py:14
  156.5 15.5 %fusion = f32[4,128,128]{2,0,1:T(4,128)S(1)} fusion(f32[128,128,128]{2,1,0:T(8,128)} %param.30, f32[128,4,128]{2,1,0:T(4,128)S(1)} %gather_fusion.1, f32[128,128]{1,0:T(8,128)S(1)} %broadcast_multiply_fusion, pred[128]{0:T(512)(128)(4,1)S(1)} %compare_and_fusion), kind=kOutput, calls=%fused_computation.3 | convolution fusion | flops 100794368 | bytes 8978560 | tf_op jit(solution)/shard_map/bij,pbj->pbi/dot_general | solution.py:92
  172.0 9.4 %fusion.93 = f32[128,4,128]{2,1,0:T(4,128)S(1)} fusion(f32[4,128,128]{2,0,1:T(4,128)S(1)} %fusion, f32[128,128,128]{2,1,0:T(8,128)} %param.30), kind=kOutput, calls=%fused_computation.210 | convolution fusion | flops 100663296 | bytes 8912896 | tf_op jit(solution)/shard_map/bij,pbi->pbj/dot_general | solution.py:100
  181.9 3.9 %collective-permute-start.28 = (f32[4,384]{1,0:T(4,128)S(1)}, f32[4,384]{1,0:T(4,128)S(1)}, u32[]{:S(2)}, u32[]{:S(2)}) collective-permute-start(f32[4,384]{1,0:T(4,128)S(1)} %pad_maximum_fusion.76), channel_id=1, source_target_pairs={{0,4},{4,8},{8,12},{1,5},{5,9},{9,13},{2,6},{6,10},{10,14},{3,7},{... | collective-permute-start | bytes 18440 | tf_op jit(solution)/shard_map/ppermute | solution.py:25
  185.8 4.6 %collective-permute-start.21 = (f32[4,34,1]{2,0,1:T(4,128)S(1)}, f32[4,34,1]{2,0,1:T(4,128)S(1)}, u32[]{:S(2)}, u32[]{:S(2)}) collective-permute-start(f32[4,34,1]{2,0,1:T(4,128)S(1)} %get-tuple-element.131), channel_id=1, source_target_pairs={{0,2},{1,3},{4,6},{5,7},{8,10},{9,11},{12,14},{13,15},{16,18},{17,... | collective-permute-start | bytes 1640 | tf_op jit(solution)/shard_map/ppermute | solution.py:14
  190.4 1.3 collective-permute-start.20
  192.3 4.3 %collective-permute-done.20 = f32[4,34,1]{2,0,1:T(4,128)S(1)} collective-permute-done((f32[4,34,1]{2,0,1:T(4,128)S(1)}, f32[4,34,1]{2,0,1:T(4,128)S(1)}, u32[]{:S(2)}, u32[]{:S(2)}) %collective-permute-start.20) | collective-permute-done | bytes 576 | tf_op jit(solution)/shard_map/ppermute | solution.py:17
  196.8 1.3 collective-permute-start.22
  198.1 4.5 %collective-permute-start.23 = (f32[4,1,256]{2,0,1:T(4,128)S(1)}, f32[4,1,256]{2,0,1:T(4,128)S(1)}, u32[]{:S(2)}, u32[]{:S(2)}) collective-permute-start(f32[4,1,256]{2,0,1:T(4,128)S(1)} %get-tuple-element.140), channel_id=1, source_target_pairs={{0,4},{4,8},{8,12},{1,5},{5,9},{9,13},{2,6},{6,10},{10,14},{3,7},{... | collective-permute-start | bytes 12296 | tf_op jit(solution)/shard_map/ppermute | solution.py:14
  202.8 1.6 collective-permute-start.35
  204.3 1.3 collective-permute-start.34
  205.8 4.5 %collective-permute-start.25 = (f32[4,34,1]{2,0,1:T(4,128)S(1)}, f32[4,34,1]{2,0,1:T(4,128)S(1)}, u32[]{:S(2)}, u32[]{:S(2)}) collective-permute-start(f32[4,34,1]{2,0,1:T(4,128)S(1)} %get-tuple-element.129), channel_id=1, source_target_pairs={{0,2},{1,3},{4,6},{5,7},{8,10},{9,11},{12,14},{13,15},{16,18},{17,... | collective-permute-start | bytes 1640 | tf_op jit(solution)/shard_map/ppermute | solution.py:14
  210.4 1.3 collective-permute-start.24
  211.7 1.3 collective-permute-start.29
  213.0 4.2 %collective-permute-done.29 = f32[4,384]{1,0:T(4,128)S(1)} collective-permute-done((f32[4,384]{1,0:T(4,128)S(1)}, f32[4,384]{1,0:T(4,128)S(1)}, u32[]{:S(2)}, u32[]{:S(2)}) %collective-permute-start.29) | collective-permute-done | bytes 6176 | tf_op jit(solution)/shard_map/ppermute | solution.py:25
  217.9 19.8 %psum.31 = f32[4]{0:T(128)S(1)} all-reduce(f32[4]{0:T(128)S(1)} %add.235), channel_id=1, replica_groups=mesh['grp'=2,'ew'=4,'ns'=2,'lvl'=2] {'ew','ns'}, use_global_device_ids=true, to_apply=%region_11.13 | all-reduce | flops 4 | bytes 32 | tf_op jit(solution)/shard_map/psum | solution.py:124
  (138 shorter events, 16.5 us)
Async XLA Ops:
  1.4 18.1 %collective-permute-start.9 = (f32[4,1,128]{2,1,0:T(1,128)S(1)}, f32[4,1,128]{2,1,0:T(1,128)S(1)}, u32[]{:S(2)}, u32[]{:S(2)}) collective-permute-start(f32[4,1,128]{2,1,0:T(1,128)S(1)} %get-tuple-element.165), channel_id=1, source_target_pairs={{4,0},{8,4},{12,8},{5,1},{9,5},{13,9},{6,2},{10,6},{14,10},{7,3},{... | collective-permute-start | bytes 6152 | tf_op jit(solution)/shard_map/ppermute | solution.py:17
  2.7 16.8 %collective-permute-start.8 = (f32[4,1,128]{2,1,0:T(1,128)S(1)}, f32[4,1,128]{2,1,0:T(1,128)S(1)}, u32[]{:S(2)}, u32[]{:S(2)}) collective-permute-start(f32[4,1,128]{2,1,0:T(1,128)S(1)} %get-tuple-element.164), channel_id=1, source_target_pairs={{0,4},{4,8},{8,12},{1,5},{5,9},{9,13},{2,6},{6,10},{10,14},{3,7},{... | collective-permute-start | bytes 6152 | tf_op jit(solution)/shard_map/ppermute | solution.py:14
  9.3 26.1 %collective-permute-start = (f32[4,1,256]{2,0,1:T(4,128)S(1)}, f32[4,1,256]{2,0,1:T(4,128)S(1)}, u32[]{:S(2)}, u32[]{:S(2)}) collective-permute-start(f32[4,1,256]{2,0,1:T(4,128)S(1)} %get-tuple-element.147), channel_id=1, source_target_pairs={{4,0},{8,4},{12,8},{5,1},{9,5},{13,9},{6,2},{10,6},{14,10},{7,3},{... | collective-permute-start | bytes 12296 | tf_op jit(solution)/shard_map/ppermute | solution.py:17
  10.6 24.8 %collective-permute-start.1 = (f32[4,1,256]{2,0,1:T(4,128)S(1)}, f32[4,1,256]{2,0,1:T(4,128)S(1)}, u32[]{:S(2)}, u32[]{:S(2)}) collective-permute-start(f32[4,1,256]{2,0,1:T(4,128)S(1)} %get-tuple-element.146), channel_id=1, source_target_pairs={{0,4},{4,8},{8,12},{1,5},{5,9},{9,13},{2,6},{6,10},{10,14},{3,7},{... | collective-permute-start | bytes 12296 | tf_op jit(solution)/shard_map/ppermute | solution.py:14
  19.6 5.6 %collective-permute-start.13 = (f32[4,18,1]{2,1,0:T(8,128)S(1)}, f32[4,18,1]{2,1,0:T(8,128)S(1)}, u32[]{:S(2)}, u32[]{:S(2)}) collective-permute-start(f32[4,18,1]{2,1,0:T(8,128)S(1)} %get-tuple-element.155), channel_id=1, source_target_pairs={{0,2},{1,3},{4,6},{5,7},{8,10},{9,11},{12,14},{13,15},{16,18},{17,... | collective-permute-start | bytes 872 | tf_op jit(solution)/shard_map/ppermute | solution.py:14
  23.5 6.0 %collective-permute-start.12 = (f32[4,18,1]{2,1,0:T(8,128)S(1)}, f32[4,18,1]{2,1,0:T(8,128)S(1)}, u32[]{:S(2)}, u32[]{:S(2)}) collective-permute-start(f32[4,18,1]{2,1,0:T(8,128)S(1)} %get-tuple-element.154), channel_id=1, source_target_pairs={{2,0},{3,1},{6,4},{7,5},{10,8},{11,9},{14,12},{15,13},{18,16},{19,... | collective-permute-start | bytes 872 | tf_op jit(solution)/shard_map/ppermute | solution.py:17
  29.6 37.6 %collective-permute-start.14 = (f32[4,1,128]{2,1,0:T(1,128)S(1)}, f32[4,1,128]{2,1,0:T(1,128)S(1)}, u32[]{:S(2)}, u32[]{:S(2)}) collective-permute-start(f32[4,1,128]{2,1,0:T(1,128)S(1)} %get-tuple-element.163), channel_id=1, source_target_pairs={{4,0},{8,4},{12,8},{5,1},{9,5},{13,9},{6,2},{10,6},{14,10},{7,3},{... | collective-permute-start | bytes 6152 | tf_op jit(solution)/shard_map/ppermute | solution.py:17
  30.9 36.3 %collective-permute-start.15 = (f32[4,1,128]{2,1,0:T(1,128)S(1)}, f32[4,1,128]{2,1,0:T(1,128)S(1)}, u32[]{:S(2)}, u32[]{:S(2)}) collective-permute-start(f32[4,1,128]{2,1,0:T(1,128)S(1)} %get-tuple-element.162), channel_id=1, source_target_pairs={{0,4},{4,8},{8,12},{1,5},{5,9},{9,13},{2,6},{6,10},{10,14},{3,7},{... | collective-permute-start | bytes 6152 | tf_op jit(solution)/shard_map/ppermute | solution.py:14
  36.3 16.4 %copy-start = (f32[128,128,128]{2,1,0:T(8,128)S(1)}, f32[128,128,128]{2,1,0:T(8,128)}, u32[]{:S(2)}) copy-start(f32[128,128,128]{2,1,0:T(8,128)} %param.30) | copy-start | bytes 25165828
  36.3 23.7 %copy-start.3 = (s32[128]{0:T(128)S(1)}, s32[128]{0:T(128)}, u32[]{:S(2)}) copy-start(s32[128]{0:T(128)} %param.32) | copy-start | bytes 1540
  36.3 56.5 %copy-start.1 = (s32[4,32,256]{2,1,0:T(8,128)S(1)}, s32[4,32,256]{2,1,0:T(8,128)}, u32[]{:S(2)}) copy-start(s32[4,32,256]{2,1,0:T(8,128)} %param.26) | copy-start | bytes 393220
  52.7 40.5 %copy-start.2 = (s32[4,16,128]{2,1,0:T(8,128)S(1)}, s32[4,16,128]{2,1,0:T(8,128)}, u32[]{:S(2)}) copy-start(s32[4,16,128]{2,1,0:T(8,128)} %param.27) | copy-start | bytes 98308
  60.6 26.6 %collective-permute-start.10 = (f32[4,384]{1,0:T(4,128)S(1)}, f32[4,384]{1,0:T(4,128)S(1)}, u32[]{:S(2)}, u32[]{:S(2)}) collective-permute-start(f32[4,384]{1,0:T(4,128)S(1)} %pad_maximum_fusion.74), channel_id=1, source_target_pairs={{0,4},{4,8},{8,12},{1,5},{5,9},{9,13},{2,6},{6,10},{10,14},{3,7},{... | collective-permute-start | bytes 18440 | tf_op jit(solution)/shard_map/ppermute | solution.py:25
  64.1 3.5 %collective-permute-start.3 = (f32[4,34,1]{2,0,1:T(4,128)S(1)}, f32[4,34,1]{2,0,1:T(4,128)S(1)}, u32[]{:S(2)}, u32[]{:S(2)}) collective-permute-start(f32[4,34,1]{2,0,1:T(4,128)S(1)} %get-tuple-element.137), channel_id=1, source_target_pairs={{0,2},{1,3},{4,6},{5,7},{8,10},{9,11},{12,14},{13,15},{16,18},{17,... | collective-permute-start | bytes 1640 | tf_op jit(solution)/shard_map/ppermute | solution.py:14
  65.7 6.4 %collective-permute-start.2 = (f32[4,34,1]{2,0,1:T(4,128)S(1)}, f32[4,34,1]{2,0,1:T(4,128)S(1)}, u32[]{:S(2)}, u32[]{:S(2)}) collective-permute-start(f32[4,34,1]{2,0,1:T(4,128)S(1)} %get-tuple-element.136), channel_id=1, source_target_pairs={{2,0},{3,1},{6,4},{7,5},{10,8},{11,9},{14,12},{15,13},{18,16},{19,... | collective-permute-start | bytes 1640 | tf_op jit(solution)/shard_map/ppermute | solution.py:17
  72.4 8.8 %collective-permute-start.4 = (f32[4,1,256]{2,0,1:T(4,128)S(1)}, f32[4,1,256]{2,0,1:T(4,128)S(1)}, u32[]{:S(2)}, u32[]{:S(2)}) collective-permute-start(f32[4,1,256]{2,0,1:T(4,128)S(1)} %get-tuple-element.145), channel_id=1, source_target_pairs={{4,0},{8,4},{12,8},{5,1},{9,5},{13,9},{6,2},{10,6},{14,10},{7,3},{... | collective-permute-start | bytes 12296 | tf_op jit(solution)/shard_map/ppermute | solution.py:17
  73.7 7.5 %collective-permute-start.5 = (f32[4,1,256]{2,0,1:T(4,128)S(1)}, f32[4,1,256]{2,0,1:T(4,128)S(1)}, u32[]{:S(2)}, u32[]{:S(2)}) collective-permute-start(f32[4,1,256]{2,0,1:T(4,128)S(1)} %get-tuple-element.144), channel_id=1, source_target_pairs={{0,4},{4,8},{8,12},{1,5},{5,9},{9,13},{2,6},{6,10},{10,14},{3,7},{... | collective-permute-start | bytes 12296 | tf_op jit(solution)/shard_map/ppermute | solution.py:14
  78.3 14.9 %collective-permute-start.17 = (f32[4,18,1]{2,1,0:T(8,128)S(1)}, f32[4,18,1]{2,1,0:T(8,128)S(1)}, u32[]{:S(2)}, u32[]{:S(2)}) collective-permute-start(f32[4,18,1]{2,1,0:T(8,128)S(1)} %get-tuple-element.153), channel_id=1, source_target_pairs={{0,2},{1,3},{4,6},{5,7},{8,10},{9,11},{12,14},{13,15},{16,18},{17,... | collective-permute-start | bytes 872 | tf_op jit(solution)/shard_map/ppermute | solution.py:14
  79.9 13.4 %collective-permute-start.16 = (f32[4,18,1]{2,1,0:T(8,128)S(1)}, f32[4,18,1]{2,1,0:T(8,128)S(1)}, u32[]{:S(2)}, u32[]{:S(2)}) collective-permute-start(f32[4,18,1]{2,1,0:T(8,128)S(1)} %get-tuple-element.152), channel_id=1, source_target_pairs={{2,0},{3,1},{6,4},{7,5},{10,8},{11,9},{14,12},{15,13},{18,16},{19,... | collective-permute-start | bytes 872 | tf_op jit(solution)/shard_map/ppermute | solution.py:17
  81.3 11.4 %collective-permute-start.7 = (f32[4,34,1]{2,0,1:T(4,128)S(1)}, f32[4,34,1]{2,0,1:T(4,128)S(1)}, u32[]{:S(2)}, u32[]{:S(2)}) collective-permute-start(f32[4,34,1]{2,0,1:T(4,128)S(1)} %get-tuple-element.135), channel_id=1, source_target_pairs={{0,2},{1,3},{4,6},{5,7},{8,10},{9,11},{12,14},{13,15},{16,18},{17,... | collective-permute-start | bytes 1640 | tf_op jit(solution)/shard_map/ppermute | solution.py:14
  85.9 6.9 %collective-permute-start.6 = (f32[4,34,1]{2,0,1:T(4,128)S(1)}, f32[4,34,1]{2,0,1:T(4,128)S(1)}, u32[]{:S(2)}, u32[]{:S(2)}) collective-permute-start(f32[4,34,1]{2,0,1:T(4,128)S(1)} %get-tuple-element.134), channel_id=1, source_target_pairs={{2,0},{3,1},{6,4},{7,5},{10,8},{11,9},{14,12},{15,13},{18,16},{19,... | collective-permute-start | bytes 1640 | tf_op jit(solution)/shard_map/ppermute | solution.py:17
  87.2 5.5 %collective-permute-start.11 = (f32[4,384]{1,0:T(4,128)S(1)}, f32[4,384]{1,0:T(4,128)S(1)}, u32[]{:S(2)}, u32[]{:S(2)}) collective-permute-start(f32[4,384]{1,0:T(4,128)S(1)} %pad_maximum_fusion.75), channel_id=1, source_target_pairs={{4,0},{8,4},{12,8},{5,1},{9,5},{13,9},{6,2},{10,6},{14,10},{7,3},{... | collective-permute-start | bytes 18440 | tf_op jit(solution)/shard_map/ppermute | solution.py:25
  131.2 5.9 %collective-permute-start.27 = (f32[4,1,128]{2,1,0:T(1,128)S(1)}, f32[4,1,128]{2,1,0:T(1,128)S(1)}, u32[]{:S(2)}, u32[]{:S(2)}) collective-permute-start(f32[4,1,128]{2,1,0:T(1,128)S(1)} %get-tuple-element.161), channel_id=1, source_target_pairs={{4,0},{8,4},{12,8},{5,1},{9,5},{13,9},{6,2},{10,6},{14,10},{7,3},{... | collective-permute-start | bytes 6152 | tf_op jit(solution)/shard_map/ppermute | solution.py:17
  132.5 5.8 %collective-permute-start.26 = (f32[4,1,128]{2,1,0:T(1,128)S(1)}, f32[4,1,128]{2,1,0:T(1,128)S(1)}, u32[]{:S(2)}, u32[]{:S(2)}) collective-permute-start(f32[4,1,128]{2,1,0:T(1,128)S(1)} %get-tuple-element.160), channel_id=1, source_target_pairs={{0,4},{4,8},{8,12},{1,5},{5,9},{9,13},{2,6},{6,10},{10,14},{3,7},{... | collective-permute-start | bytes 6152 | tf_op jit(solution)/shard_map/ppermute | solution.py:14
  138.4 11.2 %collective-permute-start.31 = (f32[4,18,1]{2,1,0:T(8,128)S(1)}, f32[4,18,1]{2,1,0:T(8,128)S(1)}, u32[]{:S(2)}, u32[]{:S(2)}) collective-permute-start(f32[4,18,1]{2,1,0:T(8,128)S(1)} %get-tuple-element.151), channel_id=1, source_target_pairs={{0,2},{1,3},{4,6},{5,7},{8,10},{9,11},{12,14},{13,15},{16,18},{17,... | collective-permute-start | bytes 872 | tf_op jit(solution)/shard_map/ppermute | solution.py:14
  142.2 7.4 %collective-permute-start.30 = (f32[4,18,1]{2,1,0:T(8,128)S(1)}, f32[4,18,1]{2,1,0:T(8,128)S(1)}, u32[]{:S(2)}, u32[]{:S(2)}) collective-permute-start(f32[4,18,1]{2,1,0:T(8,128)S(1)} %get-tuple-element.150), channel_id=1, source_target_pairs={{2,0},{3,1},{6,4},{7,5},{10,8},{11,9},{14,12},{15,13},{18,16},{19,... | collective-permute-start | bytes 872 | tf_op jit(solution)/shard_map/ppermute | solution.py:17
  143.5 12.1 %collective-permute-start.18 = (f32[4,1,256]{2,0,1:T(4,128)S(1)}, f32[4,1,256]{2,0,1:T(4,128)S(1)}, u32[]{:S(2)}, u32[]{:S(2)}) collective-permute-start(f32[4,1,256]{2,0,1:T(4,128)S(1)} %get-tuple-element.143), channel_id=1, source_target_pairs={{4,0},{8,4},{12,8},{5,1},{9,5},{13,9},{6,2},{10,6},{14,10},{7,3},{... | collective-permute-start | bytes 12296 | tf_op jit(solution)/shard_map/ppermute | solution.py:17
  144.8 10.8 %collective-permute-start.19 = (f32[4,1,256]{2,0,1:T(4,128)S(1)}, f32[4,1,256]{2,0,1:T(4,128)S(1)}, u32[]{:S(2)}, u32[]{:S(2)}) collective-permute-start(f32[4,1,256]{2,0,1:T(4,128)S(1)} %get-tuple-element.142), channel_id=1, source_target_pairs={{0,4},{4,8},{8,12},{1,5},{5,9},{9,13},{2,6},{6,10},{10,14},{3,7},{... | collective-permute-start | bytes 12296 | tf_op jit(solution)/shard_map/ppermute | solution.py:14
  149.8 41.9 %collective-permute-start.32 = (f32[4,1,128]{2,1,0:T(1,128)S(1)}, f32[4,1,128]{2,1,0:T(1,128)S(1)}, u32[]{:S(2)}, u32[]{:S(2)}) collective-permute-start(f32[4,1,128]{2,1,0:T(1,128)S(1)} %get-tuple-element.159), channel_id=1, source_target_pairs={{4,0},{8,4},{12,8},{5,1},{9,5},{13,9},{6,2},{10,6},{14,10},{7,3},{... | collective-permute-start | bytes 6152 | tf_op jit(solution)/shard_map/ppermute | solution.py:17
  151.1 40.6 %collective-permute-start.33 = (f32[4,1,128]{2,1,0:T(1,128)S(1)}, f32[4,1,128]{2,1,0:T(1,128)S(1)}, u32[]{:S(2)}, u32[]{:S(2)}) collective-permute-start(f32[4,1,128]{2,1,0:T(1,128)S(1)} %get-tuple-element.158), channel_id=1, source_target_pairs={{0,4},{4,8},{8,12},{1,5},{5,9},{9,13},{2,6},{6,10},{10,14},{3,7},{... | collective-permute-start | bytes 6152 | tf_op jit(solution)/shard_map/ppermute | solution.py:14
  181.9 29.8 %collective-permute-start.28 = (f32[4,384]{1,0:T(4,128)S(1)}, f32[4,384]{1,0:T(4,128)S(1)}, u32[]{:S(2)}, u32[]{:S(2)}) collective-permute-start(f32[4,384]{1,0:T(4,128)S(1)} %pad_maximum_fusion.76), channel_id=1, source_target_pairs={{0,4},{4,8},{8,12},{1,5},{5,9},{9,13},{2,6},{6,10},{10,14},{3,7},{... | collective-permute-start | bytes 18440 | tf_op jit(solution)/shard_map/ppermute | solution.py:25
  185.8 6.5 %collective-permute-start.21 = (f32[4,34,1]{2,0,1:T(4,128)S(1)}, f32[4,34,1]{2,0,1:T(4,128)S(1)}, u32[]{:S(2)}, u32[]{:S(2)}) collective-permute-start(f32[4,34,1]{2,0,1:T(4,128)S(1)} %get-tuple-element.131), channel_id=1, source_target_pairs={{0,2},{1,3},{4,6},{5,7},{8,10},{9,11},{12,14},{13,15},{16,18},{17,... | collective-permute-start | bytes 1640 | tf_op jit(solution)/shard_map/ppermute | solution.py:14
  190.4 6.2 %collective-permute-start.20 = (f32[4,34,1]{2,0,1:T(4,128)S(1)}, f32[4,34,1]{2,0,1:T(4,128)S(1)}, u32[]{:S(2)}, u32[]{:S(2)}) collective-permute-start(f32[4,34,1]{2,0,1:T(4,128)S(1)} %get-tuple-element.130), channel_id=1, source_target_pairs={{2,0},{3,1},{6,4},{7,5},{10,8},{11,9},{14,12},{15,13},{18,16},{19,... | collective-permute-start | bytes 1640 | tf_op jit(solution)/shard_map/ppermute | solution.py:17
  196.8 8.8 %collective-permute-start.22 = (f32[4,1,256]{2,0,1:T(4,128)S(1)}, f32[4,1,256]{2,0,1:T(4,128)S(1)}, u32[]{:S(2)}, u32[]{:S(2)}) collective-permute-start(f32[4,1,256]{2,0,1:T(4,128)S(1)} %get-tuple-element.141), channel_id=1, source_target_pairs={{4,0},{8,4},{12,8},{5,1},{9,5},{13,9},{6,2},{10,6},{14,10},{7,3},{... | collective-permute-start | bytes 12296 | tf_op jit(solution)/shard_map/ppermute | solution.py:17
  198.1 7.5 %collective-permute-start.23 = (f32[4,1,256]{2,0,1:T(4,128)S(1)}, f32[4,1,256]{2,0,1:T(4,128)S(1)}, u32[]{:S(2)}, u32[]{:S(2)}) collective-permute-start(f32[4,1,256]{2,0,1:T(4,128)S(1)} %get-tuple-element.140), channel_id=1, source_target_pairs={{0,4},{4,8},{8,12},{1,5},{5,9},{9,13},{2,6},{6,10},{10,14},{3,7},{... | collective-permute-start | bytes 12296 | tf_op jit(solution)/shard_map/ppermute | solution.py:14
  202.8 14.9 %collective-permute-start.35 = (f32[4,18,1]{2,1,0:T(8,128)S(1)}, f32[4,18,1]{2,1,0:T(8,128)S(1)}, u32[]{:S(2)}, u32[]{:S(2)}) collective-permute-start(f32[4,18,1]{2,1,0:T(8,128)S(1)} %get-tuple-element.149), channel_id=1, source_target_pairs={{0,2},{1,3},{4,6},{5,7},{8,10},{9,11},{12,14},{13,15},{16,18},{17,... | collective-permute-start | bytes 872 | tf_op jit(solution)/shard_map/ppermute | solution.py:14
  204.3 13.3 %collective-permute-start.34 = (f32[4,18,1]{2,1,0:T(8,128)S(1)}, f32[4,18,1]{2,1,0:T(8,128)S(1)}, u32[]{:S(2)}, u32[]{:S(2)}) collective-permute-start(f32[4,18,1]{2,1,0:T(8,128)S(1)} %get-tuple-element.148), channel_id=1, source_target_pairs={{2,0},{3,1},{6,4},{7,5},{10,8},{11,9},{14,12},{15,13},{18,16},{19,... | collective-permute-start | bytes 872 | tf_op jit(solution)/shard_map/ppermute | solution.py:17
  205.8 11.4 %collective-permute-start.25 = (f32[4,34,1]{2,0,1:T(4,128)S(1)}, f32[4,34,1]{2,0,1:T(4,128)S(1)}, u32[]{:S(2)}, u32[]{:S(2)}) collective-permute-start(f32[4,34,1]{2,0,1:T(4,128)S(1)} %get-tuple-element.129), channel_id=1, source_target_pairs={{0,2},{1,3},{4,6},{5,7},{8,10},{9,11},{12,14},{13,15},{16,18},{17,... | collective-permute-start | bytes 1640 | tf_op jit(solution)/shard_map/ppermute | solution.py:14
  210.4 6.9 %collective-permute-start.24 = (f32[4,34,1]{2,0,1:T(4,128)S(1)}, f32[4,34,1]{2,0,1:T(4,128)S(1)}, u32[]{:S(2)}, u32[]{:S(2)}) collective-permute-start(f32[4,34,1]{2,0,1:T(4,128)S(1)} %get-tuple-element.128), channel_id=1, source_target_pairs={{2,0},{3,1},{6,4},{7,5},{10,8},{11,9},{14,12},{15,13},{18,16},{19,... | collective-permute-start | bytes 1640 | tf_op jit(solution)/shard_map/ppermute | solution.py:17
  211.7 5.5 %collective-permute-start.29 = (f32[4,384]{1,0:T(4,128)S(1)}, f32[4,384]{1,0:T(4,128)S(1)}, u32[]{:S(2)}, u32[]{:S(2)}) collective-permute-start(f32[4,384]{1,0:T(4,128)S(1)} %pad_maximum_fusion.77), channel_id=1, source_target_pairs={{4,0},{8,4},{12,8},{5,1},{9,5},{13,9},{6,2},{10,6},{14,10},{7,3},{... | collective-permute-start | bytes 18440 | tf_op jit(solution)/shard_map/ppermute | solution.py:25
where the time goes:
time: 241 us; the launch traced here: 240 us
  starting transfers between devices  94.5 us (39%)
  blocking collectives  56.8 us (24%)
  matrix products  49 us (20%)
  waiting for transfers between devices  24 us (10%)
  other arithmetic  9.25 us (4%)
  local copies, waits for them, and re-layouts  4.04 us (2%)
    ppermute x16, starting transfers between devices, with_halo(): lax.ppermute(lax.slice_in_dim(block, block.shape[dim] - width, None, axis...  63.6 us
    psum x2, blocking collectives, squares(): lax.psum(local_products(first_fine, first_coarse, first_fine, first_coars...  37 us
    dot_general x2, matrix products, local(): jnp.einsum('bij,pbj->pbi', phi_tiles, picked, precision=lax.Precision.HIG...  31.8 us
    ppermute x16, starting transfers between devices, with_halo(): lax.ppermute(lax.slice_in_dim(block, 0, width, axis=dim), axis, backward)  20.9 us
    psum x1, blocking collectives, local(): lax.psum(local_products(direction_fine, direction_coarse, image_fine, ima...  19.8 us
    dot_general x2, matrix products, local(): jnp.einsum('bij,pbi->pbj', phi_tiles, scaled, precision=lax.Precision.HIG...  16.7 us
    ppermute x16, waiting for transfers between devices, with_halo(): lax.ppermute(lax.slice_in_dim(block, 0, width, axis=dim), axis, backward)  13 us
    ppermute x4, starting transfers between devices, shifted(): return lax.ppermute(block, axis, route)  9.99 us
  transfers between devices with their start and end apart: 36, of which 9 were waited for; matrix products, arithmetic and copies ran while one was open for 24% of the time, Pallas kernels for 0%

commit v1 on v0

v1 whole, which is shorter than its diff:
```python
import functools

import jax
import jax.numpy as jnp
from jax import lax
from jax.experimental import pallas as pl
from jax.experimental.pallas import tpu as pltpu
from jax.sharding import PartitionSpec as P

MESH = pl.DeviceIdType.MESH
CHUNKS = 16
GROUP = 8
F32 = jnp.float32
BF16 = jnp.bfloat16


def kernel(
    n_ew,
    n_ns,
    pf_ref,
    pc_ref,
    kf_ref,
    kc_ref,
    phi_ref,
    wt_ref,
    idxv_ref,
    cnt_ref,
    xf_ref,
    xc_ref,
    rf_ref,
    rc_ref,
    phi32,
    ph,
    z,
    u0,
    q1,
    u1,
    adj,
    im,
    ext,
    back,
    wm,
    onehot,
    pick,
    row_out,
    row_in,
    col_in,
    ar_out,
    ar_in,
    phi_sem,
    row_ssem,
    row_rsem,
    col_ssem,
    col_rsem,
    ar_ssem,
    ar_rsem,
):
    probes, rows, width = pf_ref.shape
    half_rows = pc_ref.shape[1]
    tile = pc_ref.shape[2]
    blocks = ph.shape[0]
    at = (8, rows + 24, rows + half_rows + 40)
    size = (rows, half_rows, rows)
    total = n_ew * n_ns
    e = lax.axis_index("ew")
    n = lax.axis_index("ns")
    me = e * n_ns + n
    has_row = (e > 0, e < n_ew - 1)
    has_col = (n > 0, n < n_ns - 1)
    row_dev = ({"ew": lax.max(e - 1, 0)}, {"ew": lax.min(e + 1, n_ew - 1)})
    col_dev = ({"ns": lax.max(n - 1, 0)}, {"ns": lax.min(n + 1, n_ns - 1)})

    def phi_copy(c):
        step = blocks // CHUNKS
        return pltpu.make_async_copy(
            phi_ref.at[pl.ds(c * step, step)], phi32.at[pl.ds(c * step, step)], phi_sem.at[c]
        )

    def start_phi(c, _):
        phi_copy(c).start()
        return 0

    lax.fori_loop(0, CHUNKS, start_phi, 0)

    def peer(k):
        other = lax.rem(me + k, total)
        return {"ew": other // n_ns, "ns": lax.rem(other, n_ns)}

    barrier = pltpu.get_barrier_semaphore()
    for k in range(1, total):
        pl.semaphore_signal(barrier, inc=1, device_id=peer(k), device_id_type=MESH)

    z[...] = jnp.zeros_like(z)
    u0[...] = jnp.zeros_like(u0)
    q1[...] = jnp.zeros_like(q1)
    u1[...] = jnp.zeros_like(u1)
    fine = (2 * pf_ref[...] - 1).astype(F32)
    z[:, at[0] : at[0] + rows, :] = fine[:, :, :tile]
    z[:, at[2] : at[2] + rows, :] = fine[:, :, tile:]
    z[:, at[1] : at[1] + half_rows, :] = (2 * pc_ref[...] - 1).astype(F32)
    row_out[...] = jnp.zeros_like(row_out)
    ar_out[...] = jnp.zeros_like(ar_out)
    for d in range(2):

        @pl.when(jnp.logical_not(has_row[d]))
        def _():
            for k in range(5):
                row_in[k, d] = jnp.zeros(row_in.shape[2:], F32)

        @pl.when(jnp.logical_not(has_col[d]))
        def _():
            for k in range(4):
                col_in[k, d] = jnp.zeros(col_in.shape[2:], F32)

    def row_copy(k, d):
        return pltpu.make_async_remote_copy(
            src_ref=row_out.at[k, d],
            dst_ref=row_in.at[k, 1 - d],
            send_sem=row_ssem.at[k, d],
            recv_sem=row_rsem.at[k, 1 - d],
            device_id=row_dev[d],
            device_id_type=MESH,
        )

    def row_start(k):
        for d in range(2):

            @pl.when(has_row[d])
            def _():
                row_copy(k, d).start()

    def row_wait(k):
        for d in range(2):

            @pl.when(has_row[d])
            def _():
                row_copy(k, 1 - d).wait_recv()

    def col_copies(field, k, d):
        seg = 0 if d == 0 else 2
        out = []
        for j, (s, first) in enumerate(((seg, 0), (1, rows))):
            out.append(
                pltpu.make_async_remote_copy(
                    src_ref=field.at[:, pl.ds(at[s], size[s]), :],
                    dst_ref=col_in.at[k, 1 - d, :, pl.ds(first, size[s]), :],
                    send_sem=col_ssem.at[k, d, j],
                    recv_sem=col_rsem.at[k, 1 - d, j],
                    device_id=col_dev[d],
                    device_id_type=MESH,
                )
            )
        return out

    def col_start(field, k):
        for d in range(2):

            @pl.when(has_col[d])
            def _():
                for c in col_copies(field, k, d):
                    c.start()

    def col_wait(field, k):
        for d in range(2):

            @pl.when(has_col[d])
            def _():
                for c in col_copies(field, k, 1 - d):
                    c.wait_recv()

    def pack_rows(field, k, first=0, outside=False):
        for s in range(3):
            low, high = at[s], at[s] + size[s] - 1
            if outside:
                low, high = low - 1, high + 1
            for p in range(probes):
                row_out[k, 0, s, pl.ds(first + p, 1), :] = field[p, pl.ds(low, 1), :]
                row_out[k, 1, s, pl.ds(first + p, 1), :] = field[p, pl.ds(high, 1), :]

    def unpack_rows(field, k):
        for s in range(3):
            for p in range(probes):
                field[p, pl.ds(at[s] - 1, 1), :] = row_in[k, 0, s, pl.ds(p, 1), :]
                field[p, pl.ds(at[s] + size[s], 1), :] = row_in[k, 1, s, pl.ds(p, 1), :]

    def sar(field, k, s, p):
        lane = lax.broadcasted_iota(jnp.int32, (size[s], tile), 1)

        def seg(which):
            return field[p, pl.ds(at[which], size[which]), :]

        first, last = (0, rows) if s != 1 else (rows, rows + half_rows)
        low = seg(0) if s == 2 else col_in[k, 0, p, first:last, :]
        high = seg(2) if s == 0 else col_in[k, 1, p, first:last, :]
        centre = seg(s)
        left = jnp.where(lane == 0, pltpu.roll(low, 1, 1), pltpu.roll(centre, 1, 1))
        right = jnp.where(
            lane == tile - 1, pltpu.roll(high, tile - 1, 1), pltpu.roll(centre, tile - 1, 1)
        )
        up = field[p, pl.ds(at[s] - 1, size[s]), :]
        down = field[p, pl.ds(at[s] + 1, size[s]), :]
        kap = kc_ref[...] if s == 1 else kf_ref[:, (s // 2) * tile : (s // 2 + 1) * tile]
        return (4.0 + kap) * centre - (down + up + right + left)

    def own(field, p, s):
        return field[p, pl.ds(at[s], size[s]), :]

    def put(field, p, s, value):
        field[p, pl.ds(at[s], size[s]), :] = value

    pl.semaphore_wait(barrier, total - 1)
    pack_rows(z, 0)
    row_start(0)
    col_start(z, 0)

    alive = lax.broadcasted_iota(jnp.int32, (blocks, tile), 0) < cnt_ref[0]
    wm[...] = jnp.where(alive, wt_ref[...], 0.0)
    line = lax.broadcasted_iota(jnp.int32, (z.shape[1], blocks), 0)
    per_row = width // tile
    name = jnp.where(
        line <= at[0] + rows,
        per_row * (line - (at[0] - 1)),
        jnp.where(
            line <= at[1] + half_rows,
            (rows + 2) * per_row + line - (at[1] - 1),
            per_row * (line - (at[2] - 1)) + 1,
        ),
    )
    inside = (
        ((line >= at[0] - 1) & (line <= at[0] + rows))
        | ((line >= at[1] - 1) & (line <= at[1] + half_rows))
        | ((line >= at[2] - 1) & (line <= at[2] + rows))
    )
    chosen = jnp.where(inside & (name == idxv_ref[...]), 1.0, 0.0)
    onehot[...] = chosen.astype(BF16)
    pick[...] = chosen.T.astype(BF16)

    def split_chunk(c, _):
        step = blocks // CHUNKS
        phi_copy(c).wait()
        for k in range(step):
            x = phi32[c * step + k]
            hi = x.astype(BF16)
            ph[c * step + k, 0:tile, :] = hi
            ph[c * step + k, tile : 2 * tile, :] = (x - hi.astype(F32)).astype(BF16)
        return 0

    lax.fori_loop(0, CHUNKS, split_chunk, 0)

    def fill_ext(field):
        for p in range(probes):
            x = field[p]
            hi = x.astype(BF16)
            lo = (x - hi.astype(F32)).astype(BF16)
            out = jnp.dot(
                pick[...], jnp.concatenate([hi, lo], axis=1), preferred_element_type=F32
            )
            ext[pl.ds(p, blocks, stride=8), :] = out[:, :tile]
            ext[pl.ds(4 + p, blocks, stride=8), :] = out[:, tile:]

    top = lax.broadcasted_iota(jnp.int32, (8, tile), 0) < 4

    def observe(g, _):
        scaled = []
        for k in range(GROUP):
            b = g * GROUP + k
            got = ext[pl.ds(pl.multiple_of(b * 8, 8), 8), :].astype(BF16)
            seen = lax.dot_general(
                got, ph[b], (((1,), (1,)), ((), ())), preferred_element_type=F32
            )
            seen = seen[:, :tile] + seen[:, tile:]
            seen = seen + pltpu.roll(seen, 4, 0)
            scaled.append(seen * wm[pl.ds(b, 1), :])
        for k in range(GROUP):
            b = g * GROUP + k
            hi = scaled[k].astype(BF16).astype(F32)
            parts = jnp.where(top, hi, scaled[k] - hi).astype(BF16)
            out = lax.dot_general(
                jnp.concatenate([parts, parts], axis=1),
                ph[b],
                (((1,), (0,)), ((), ())),
                preferred_element_type=F32,
            )
            back[pl.ds(pl.multiple_of(b * 8, 8), 8), :] = out + pltpu.roll(out, 4, 0)
        return 0

    steps = blocks // GROUP

    def scatter():
        for p in range(probes):
            x = back[pl.ds(p, blocks, stride=8), :]
            hi = x.astype(BF16)
            lo = (x - hi.astype(F32)).astype(BF16)
            out = jnp.dot(
                onehot[...], jnp.concatenate([hi, lo], axis=1), preferred_element_type=F32
            )
            adj[p] = out[:, :tile] + out[:, tile:]

    def ar_copy(k, j):
        return pltpu.make_async_remote_copy(
            src_ref=ar_out.at[k],
            dst_ref=ar_in.at[k, me],
            send_sem=ar_ssem.at[k, j],
            recv_sem=ar_rsem.at[k, me],
            device_id=peer(j),
            device_id_type=MESH,
        )

    def ar_recv(k, j):
        other = lax.rem(me + j, total)
        return pltpu.make_async_remote_copy(
            src_ref=ar_out.at[k],
            dst_ref=ar_in.at[k, other],
            send_sem=ar_ssem.at[k, j],
            recv_sem=ar_rsem.at[k, other],
            device_id=peer(j),
            device_id_type=MESH,
        )

    def ar_start(k):
        for j in range(1, total):
            ar_copy(k, j).start()
        ar_in[k, me] = ar_out[k]

    def ar_wait(k):
        for j in range(1, total):
            ar_recv(k, j).wait_recv()
        acc = ar_in[k, 0]
        for j in range(1, total):
            acc = acc + ar_in[k, j]
        return jnp.sum(acc, axis=1, keepdims=True)

    row_wait(0)
    unpack_rows(z, 0)
    col_wait(z, 0)
    for p in range(probes):
        for s in range(3):
            put(u0, p, s, sar(z, 0, s, p))
    pack_rows(u0, 1)
    row_start(1)
    col_start(u0, 1)
    fill_ext(z)
    lax.fori_loop(0, steps, observe, 0)
    scatter()
    row_wait(1)
    unpack_rows(u0, 1)
    col_wait(u0, 1)
    for p in range(probes):
        for s in range(3):
            put(q1, p, s, sar(u0, 1, s, p) + own(adj, p, s))
    pack_rows(q1, 2)
    pack_rows(adj, 2, first=4, outside=True)
    row_start(2)
    row_wait(2)
    mask = [jnp.where(h, 1.0, 0.0) for h in has_row]
    for s in range(3):
        edge = (at[s] - 1, at[s] + size[s])
        inner = (at[s], at[s] + size[s] - 1)
        for p in range(probes):
            for d in range(2):
                q1[p, pl.ds(edge[d], 1), :] = (
                    row_in[2, d, s, pl.ds(p, 1), :] + adj[p, pl.ds(edge[d], 1), :] * mask[d]
                )
                q1[p, pl.ds(inner[d], 1), :] = (
                    q1[p, pl.ds(inner[d], 1), :] + row_in[2, d, s, pl.ds(4 + p, 1), :]
                )
    col_start(q1, 2)

    def lanes(first, second, p):
        out = None
        for s in range(3):
            part = jnp.sum(first(p, s) * second(p, s), axis=0, keepdims=True)
            out = part if out is None else out + part
        return out

    own_z = functools.partial(own, z)
    own_q = functools.partial(own, q1)
    for p in range(probes):
        ar_out[0, pl.ds(p, 1), :] = lanes(own_z, own_z, p)
        ar_out[0, pl.ds(4 + p, 1), :] = lanes(own_z, own_q, p)
        ar_out[0, pl.ds(8 + p, 1), :] = lanes(own_q, own_q, p)
    ar_start(0)

    fill_ext(q1)
    lax.fori_loop(0, steps // 2, observe, 0)
    col_wait(q1, 2)
    for p in range(probes):
        for s in range(3):
            put(u1, p, s, sar(q1, 2, s, p))
    pack_rows(u1, 3)
    row_start(3)
    col_start(u1, 3)
    lax.fori_loop(steps // 2, steps, observe, 0)
    scatter()
    pack_rows(adj, 4, outside=True)
    row_start(4)
    row_wait(3)
    unpack_rows(u1, 3)
    col_wait(u1, 3)
    sums = ar_wait(0)
    rr, pq, qq = sums[0:4], sums[4:8], sums[8:12]
    alpha = rr / pq
    grow = alpha * (qq / pq)
    for p in range(probes):
        a1, g1 = alpha[p : p + 1], grow[p : p + 1]
        line_sum, norm_sum = None, None
        for s in range(3):
            image = g1 * own(q1, p, s) - a1 * (sar(u1, 3, s, p) + own(adj, p, s))
            direction = g1 * own(z, p, s) - a1 * own(q1, p, s)
            part = jnp.sum(direction * image, axis=0, keepdims=True)
            for d in range(2):
                edge = (at[s] - 1, at[s] + size[s])[d]
                outside = g1 * z[p, pl.ds(edge, 1), :] - a1 * q1[p, pl.ds(edge, 1), :]
                part = part - a1 * (outside * adj[p, pl.ds(edge, 1), :]) * mask[d]
            line_sum = part if line_sum is None else line_sum + part
            resid = own(z, p, s) - a1 * own(q1, p, s)
            part = jnp.sum(resid * resid, axis=0, keepdims=True)
            norm_sum = part if norm_sum is None else norm_sum + part
            put(im, p, s, image)
        ar_out[1, pl.ds(p, 1), :] = line_sum
        ar_out[1, pl.ds(4 + p, 1), :] = norm_sum
    ar_start(1)

    row_wait(4)
    for s in range(3):
        inner = (at[s], at[s] + size[s] - 1)
        for p in range(probes):
            for d in range(2):
                im[p, pl.ds(inner[d], 1), :] = (
                    im[p, pl.ds(inner[d], 1), :]
                    - alpha[p : p + 1] * row_in[4, d, s, pl.ds(p, 1), :]
                )
    last = ar_wait(1)
    alpha_two = last[4:8] / last[0:4]
    for p in range(probes):
        a1, g1, a2 = alpha[p : p + 1], grow[p : p + 1], alpha_two[p : p + 1]
        for s in range(3):
            zz, qq_ = own(z, p, s), own(q1, p, s)
            solve = a1 * zz + a2 * (g1 * zz - a1 * qq_)
            resid = zz - a1 * qq_ - a2 * own(im, p, s)
            if s == 1:
                xc_ref[p] = solve
                rc_ref[p] = resid
            else:
                columns = slice((s // 2) * tile, (s // 2 + 1) * tile)
                xf_ref[p, :, columns] = solve
                rf_ref[p, :, columns] = resid
    for k in range(5):
        for d in range(2):

            @pl.when(has_row[d])
            def _():
                row_copy(k, d).wait_send()

    for k, field in enumerate((z, u0, q1, u1)):
        for d in range(2):

            @pl.when(has_col[d])
            def _():
                for c in col_copies(field, k, d):
                    c.wait_send()

    for k in range(2):
        for j in range(1, total):
            ar_copy(k, j).wait_send()


def local(
    n_ew,
    n_ns,
    probe_fine,
    probe_coarse,
    kappa_fine,
    kappa_coarse,
    phi_tiles,
    obs_weight,
    block_index,
    block_count,
):
    probes, rows, width = probe_fine.shape
    half_rows, tile = probe_coarse.shape[1:]
    blocks = phi_tiles.shape[0]
    lines = 2 * rows + half_rows + 48
    total = n_ew * n_ns
    vmem = pl.BlockSpec(memory_space=pltpu.VMEM)
    smem = pl.BlockSpec(memory_space=pltpu.SMEM)
    field = pltpu.VMEM((probes, lines, tile), F32)
    dma = pltpu.SemaphoreType.DMA
    return pl.pallas_call(
        functools.partial(kernel, n_ew, n_ns),
        out_shape=(
            jax.ShapeDtypeStruct(probe_fine.shape, F32),
            jax.ShapeDtypeStruct(probe_coarse.shape, F32),
            jax.ShapeDtypeStruct(probe_fine.shape, F32),
            jax.ShapeDtypeStruct(probe_coarse.shape, F32),
        ),
        in_specs=[vmem] * 4 + [pl.BlockSpec(memory_space=pl.ANY), vmem, vmem, smem],
        out_specs=(vmem,) * 4,
        scratch_shapes=[
            pltpu.VMEM(phi_tiles.shape, F32),
            pltpu.VMEM((blocks, 2 * tile, tile), BF16),
            field,
            field,
            field,
            field,
            field,
            field,
            pltpu.VMEM((blocks * 8, tile), F32),
            pltpu.VMEM((blocks * 8, tile), F32),
            pltpu.VMEM((blocks, tile), F32),
            pltpu.VMEM((lines, blocks), BF16),
            pltpu.VMEM((blocks, lines), BF16),
            pltpu.VMEM((5, 2, 3, 8, tile), F32),
            pltpu.VMEM((5, 2, 3, 8, tile), F32),
            pltpu.VMEM((4, 2, probes, rows + half_rows, tile), F32),
            pltpu.VMEM((2, 16, tile), F32),
            pltpu.VMEM((2, total, 16, tile), F32),
            dma((CHUNKS,)),
            dma((5, 2)),
            dma((5, 2)),
            dma((4, 2, 2)),
            dma((4, 2, 2)),
            dma((2, total)),
            dma((2, total)),
        ],
        compiler_params=pltpu.CompilerParams(
            collective_id=0, has_side_effects=True, vmem_limit_bytes=40 * 2**20
        ),
        cost_estimate=pl.CostEstimate(
            flops=4 * blocks * tile * tile * 8 * 4, bytes_accessed=phi_tiles.size * 4, transcendentals=0
        ),
    )(
        probe_fine,
        probe_coarse,
        kappa_fine,
        kappa_coarse,
        phi_tiles,
        obs_weight,
        block_index.reshape(1, blocks),
        block_count,
    )


def solution(mesh):
    in_specs = (
        P("lvl", "ew", "ns"),
        P("lvl", "ew", "ns"),
        P(("grp", "ew"), "ns"),
        P(("grp", "ew"), "ns"),
        P(("ew", "ns"), None, None),
        P(("grp", "ew", "ns"), None),
        P(("ew", "ns")),
        P(("ew", "ns")),
    )
    out_specs = (P(("grp", "lvl"), "ew", "ns"),) * 4
    body = functools.partial(local, mesh.shape["ew"], mesh.shape["ns"])
    return jax.shard_map(body, mesh=mesh, in_specs=in_specs, out_specs=out_specs, check_vma=False)
```

time: 241 us -> 45.4 us (0.19)
  starting transfers between devices: 94.5 us -> 0 us
  blocking collectives: 56.8 us -> 0 us
  matrix products: 49 us -> 0 us
  Pallas kernels: 0 us -> 33.2 us
  waiting for transfers between devices: 24 us -> 0 us
  other arithmetic: 9.25 us -> 0 us
  local copies, waits for them, and re-layouts: 4.04 us -> 10.5 us
    ppermute x36 -> x0, starting transfers between devices: 94.5 us -> none  [the longest x16 63.6 us: with_halo(): lax.ppermute(lax.slice_in_dim(block, block.shape[dim] - width, None, axis...]
    psum x3 -> x0, blocking collectives: 56.8 us -> none  [the longest x2 37 us: squares(): lax.psum(local_products(first_fine, first_coarse, first_fine, first_coars...]
    dot_general x6 -> x0, matrix products: 49 us -> none  [the longest x2 31.8 us: local(): jnp.einsum('bij,pbj->pbi', phi_tiles, picked, precision=lax.Precision.HIG...]
    pallas_call x0 -> x1, Pallas kernels: none -> 33.2 us  [local(): pl.pallas_call(functools.partial(kernel, n_ew, n_ns), out_shape=(jax.Shap...]
    ppermute x36 -> x0, waiting for transfers between devices: 24 us -> none  [the longest x16 13 us: with_halo(): lax.ppermute(lax.slice_in_dim(block, 0, width, axis=dim), axis, backward)]
    unnamed x13 -> x18, local copies, waits for them, and re-layouts: 1.48 us -> 10.5 us
  transfers between devices with their start and end apart: 36 -> 0, of which waited for: 9 -> 0; matrix products, arithmetic and copies ran while one was open for 24% -> 0% of each run, Pallas kernels for 0% -> 0%
where the time goes in v1:
time: 45.4 us; the launch traced here: 45 us
  Pallas kernels  33.2 us (73%)
  local copies, waits for them, and re-layouts  10.5 us (23%)
  between operations  1.3 us (3%)
    pallas_call x1, Pallas kernels, local(): pl.pallas_call(functools.partial(kernel, n_ew, n_ns), out_shape=(jax.Shap...  33.2 us
    unnamed x18, local copies, waits for them, and re-layouts  10.5 us

profile of v1, /device:TPU:0, one launch (start us, length us, event | category | flops | bytes accessed | tf_op | source)
XLA Modules:
  0.0 45.0 jit_solution(7550746871343867100)
XLA Ops:
  1.3 0.0 copy-start
  1.3 3.4 %copy-done = f32[128,128,128]{2,1,0:T(8,128)S(1)} copy-done((f32[128,128,128]{2,1,0:T(8,128)S(1)}, f32[128,128,128]{2,1,0:T(8,128)}, u32[]{:S(2)}) %copy-start) | copy-done | bytes 8388632
  4.7 0.0 copy-start.1
  4.7 0.9 %copy-done.1 = s32[4,32,256]{2,1,0:T(8,128)S(1)} copy-done((s32[4,32,256]{2,1,0:T(8,128)S(1)}, s32[4,32,256]{2,1,0:T(8,128)}, u32[]{:S(2)}) %copy-start.1) | copy-done | bytes 131096
  5.6 0.0 copy-start.2
  5.6 0.8 %copy-done.2 = f32[128,128]{1,0:T(8,128)S(1)} copy-done((f32[128,128]{1,0:T(8,128)S(1)}, f32[128,128]{1,0:T(8,128)}, u32[]{:S(2)}) %copy-start.2) | copy-done | bytes 65560
  6.4 0.0 copy-start.3
  6.4 0.8 %copy-done.3 = s32[4,16,128]{2,1,0:T(8,128)S(1)} copy-done((s32[4,16,128]{2,1,0:T(8,128)S(1)}, s32[4,16,128]{2,1,0:T(8,128)}, u32[]{:S(2)}) %copy-start.3) | copy-done | bytes 32792
  7.2 0.0 copy-start.4
  7.2 0.8 %copy-done.4 = f32[32,256]{1,0:T(8,128)S(1)} copy-done((f32[32,256]{1,0:T(8,128)S(1)}, f32[32,256]{1,0:T(8,128)}, u32[]{:S(2)}) %copy-start.4) | copy-done | bytes 32792
  7.9 0.0 copy-start.5
  7.9 0.7 %copy-done.5 = f32[16,128]{1,0:T(8,128)S(1)} copy-done((f32[16,128]{1,0:T(8,128)S(1)}, f32[16,128]{1,0:T(8,128)}, u32[]{:S(2)}) %copy-start.5) | copy-done | bytes 8216
  8.6 0.0 copy-start.6
  8.6 0.7 %copy-done.6 = s32[128]{0:T(128)S(1)} copy-done((s32[128]{0:T(128)S(1)}, s32[128]{0:T(128)}, u32[]{:S(2)}) %copy-start.6) | copy-done | bytes 536
  9.3 33.2 %shard_map.111 = (f32[4,32,256]{2,1,0:T(8,128)S(1)}, f32[4,16,128]{2,1,0:T(8,128)S(1)}, f32[4,32,256]{2,1,0:T(8,128)S(1)}, f32[4,16,128]{2,1,0:T(8,128)S(1)}) custom-call(s32[4,32,256]{2,1,0:T(8,128)S(1)} %copy-done.1, s32[4,16,128]{2,1,0:T(8,128)S(1)} %copy-done.3, f32[32,256]{1,0:T(8,128)S(1)} %copy-done.4, f32[16,128]{1,0:T(8,128)S(1)} %copy-done.5, ...), custom_call_target="tpu_custom_call" | custom-call | flops 268435456 | bytes 8388608 | tf_op jit(solution)/shard_map/pallas_call | solution.py:489
  42.5 0.7 %copy.17 = f32[4,32,256]{2,1,0:T(8,128)} copy(f32[4,32,256]{2,1,0:T(8,128)S(1)} %get-tuple-element.8) | data formatting | bytes 262144
  43.1 0.6 %copy.18 = f32[4,16,128]{2,1,0:T(8,128)} copy(f32[4,16,128]{2,1,0:T(8,128)S(1)} %get-tuple-element.9) | data formatting | bytes 65536
  43.8 0.7 %copy.19 = f32[4,32,256]{2,1,0:T(8,128)} copy(f32[4,32,256]{2,1,0:T(8,128)S(1)} %get-tuple-element.10) | data formatting | bytes 262144
  44.4 0.6 %copy.20 = f32[4,16,128]{2,1,0:T(8,128)} copy(f32[4,16,128]{2,1,0:T(8,128)S(1)} %get-tuple-element.11) | data formatting | bytes 65536
Async XLA Ops:
  1.3 3.4 %copy-start = (f32[128,128,128]{2,1,0:T(8,128)S(1)}, f32[128,128,128]{2,1,0:T(8,128)}, u32[]{:S(2)}) copy-start(f32[128,128,128]{2,1,0:T(8,128)} %phi_ref.1) | copy-start | bytes 25165828
  4.7 0.9 %copy-start.1 = (s32[4,32,256]{2,1,0:T(8,128)S(1)}, s32[4,32,256]{2,1,0:T(8,128)}, u32[]{:S(2)}) copy-start(s32[4,32,256]{2,1,0:T(8,128)} %pf_ref.1) | copy-start | bytes 393220
  5.6 0.8 %copy-start.2 = (f32[128,128]{1,0:T(8,128)S(1)}, f32[128,128]{1,0:T(8,128)}, u32[]{:S(2)}) copy-start(f32[128,128]{1,0:T(8,128)} %wt_ref.1) | copy-start | bytes 196612
  6.4 0.8 %copy-start.3 = (s32[4,16,128]{2,1,0:T(8,128)S(1)}, s32[4,16,128]{2,1,0:T(8,128)}, u32[]{:S(2)}) copy-start(s32[4,16,128]{2,1,0:T(8,128)} %pc_ref.1) | copy-start | bytes 98308
  7.2 0.8 %copy-start.4 = (f32[32,256]{1,0:T(8,128)S(1)}, f32[32,256]{1,0:T(8,128)}, u32[]{:S(2)}) copy-start(f32[32,256]{1,0:T(8,128)} %kf_ref.1) | copy-start | bytes 98308
  7.9 0.7 %copy-start.5 = (f32[16,128]{1,0:T(8,128)S(1)}, f32[16,128]{1,0:T(8,128)}, u32[]{:S(2)}) copy-start(f32[16,128]{1,0:T(8,128)} %kc_ref.1) | copy-start | bytes 24580
  8.6 0.7 %copy-start.6 = (s32[128]{0:T(128)S(1)}, s32[128]{0:T(128)}, u32[]{:S(2)}) copy-start(s32[128]{0:T(128)} %param.14) | copy-start | bytes 1540

commit v2 on v1

--- a/solution.py
+++ b/solution.py
@@ -9,7 +9,8 @@
 
 MESH = pl.DeviceIdType.MESH
 CHUNKS = 16
-GROUP = 8
+GROUP = 16
+VMEM_BYTES = 64 * 2**20 - 2**16
 F32 = jnp.float32
 BF16 = jnp.bfloat16
 
@@ -17,18 +18,24 @@
 def kernel(
     n_ew,
     n_ns,
-    pf_ref,
-    pc_ref,
-    kf_ref,
-    kc_ref,
+    pf_hbm,
+    pc_hbm,
+    kf_hbm,
+    kc_hbm,
     phi_ref,
-    wt_ref,
-    idxv_ref,
+    wt_hbm,
+    idxv_hbm,
     cnt_ref,
     xf_ref,
     xc_ref,
     rf_ref,
     rc_ref,
+    pf_ref,
+    pc_ref,
+    kf_ref,
+    kc_ref,
+    wt_ref,
+    idxv_ref,
     phi32,
     ph,
     z,
@@ -47,6 +54,7 @@
     col_in,
     ar_out,
     ar_in,
+    in_sem,
     phi_sem,
     row_ssem,
     row_rsem,
@@ -70,6 +78,20 @@
     row_dev = ({"ew": lax.max(e - 1, 0)}, {"ew": lax.min(e + 1, n_ew - 1)})
     col_dev = ({"ns": lax.max(n - 1, 0)}, {"ns": lax.min(n + 1, n_ns - 1)})
 
+    def input_copy(k):
+        source, target = (
+            (pf_hbm, pf_ref),
+            (pc_hbm, pc_ref),
+            (wt_hbm, wt_ref),
+            (idxv_hbm, idxv_ref),
+            (kf_hbm, kf_ref),
+            (kc_hbm, kc_ref),
+        )[k]
+        return pltpu.make_async_copy(source, target, in_sem.at[k])
+
+    for k in range(6):
+        input_copy(k).start()
+
     def phi_copy(c):
         step = blocks // CHUNKS
         return pltpu.make_async_copy(
@@ -94,10 +116,6 @@
     u0[...] = jnp.zeros_like(u0)
     q1[...] = jnp.zeros_like(q1)
     u1[...] = jnp.zeros_like(u1)
-    fine = (2 * pf_ref[...] - 1).astype(F32)
-    z[:, at[0] : at[0] + rows, :] = fine[:, :, :tile]
-    z[:, at[2] : at[2] + rows, :] = fine[:, :, tile:]
-    z[:, at[1] : at[1] + half_rows, :] = (2 * pc_ref[...] - 1).astype(F32)
     row_out[...] = jnp.zeros_like(row_out)
     ar_out[...] = jnp.zeros_like(ar_out)
     for d in range(2):
@@ -208,11 +226,19 @@
     def put(field, p, s, value):
         field[p, pl.ds(at[s], size[s]), :] = value
 
+    input_copy(0).wait()
+    input_copy(1).wait()
+    fine = (2 * pf_ref[...] - 1).astype(F32)
+    z[:, at[0] : at[0] + rows, :] = fine[:, :, :tile]
+    z[:, at[2] : at[2] + rows, :] = fine[:, :, tile:]
+    z[:, at[1] : at[1] + half_rows, :] = (2 * pc_ref[...] - 1).astype(F32)
     pl.semaphore_wait(barrier, total - 1)
     pack_rows(z, 0)
     row_start(0)
     col_start(z, 0)
 
+    for k in range(2, 6):
+        input_copy(k).wait()
     alive = lax.broadcasted_iota(jnp.int32, (blocks, tile), 0) < cnt_ref[0]
     wm[...] = jnp.where(alive, wt_ref[...], 0.0)
     line = lax.broadcasted_iota(jnp.int32, (z.shape[1], blocks), 0)
@@ -465,6 +491,15 @@
             ar_copy(k, j).wait_send()
 
 
+def write_out(*refs):
+    sources, targets, sem = refs[:4], refs[4:8], refs[8]
+    copies = [pltpu.make_async_copy(sources[k], targets[k], sem.at[k]) for k in range(4)]
+    for copy in copies:
+        copy.start()
+    for copy in copies:
+        copy.wait()
+
+
 def local(
     n_ew,
     n_ns,
@@ -486,7 +521,7 @@
     smem = pl.BlockSpec(memory_space=pltpu.SMEM)
     field = pltpu.VMEM((probes, lines, tile), F32)
     dma = pltpu.SemaphoreType.DMA
-    return pl.pallas_call(
+    results = pl.pallas_call(
         functools.partial(kernel, n_ew, n_ns),
         out_shape=(
             jax.ShapeDtypeStruct(probe_fine.shape, F32),
@@ -494,9 +529,15 @@
             jax.ShapeDtypeStruct(probe_fine.shape, F32),
             jax.ShapeDtypeStruct(probe_coarse.shape, F32),
         ),
-        in_specs=[vmem] * 4 + [pl.BlockSpec(memory_space=pl.ANY), vmem, vmem, smem],
+        in_specs=[pl.BlockSpec(memory_space=pltpu.HBM)] * 7 + [smem],
         out_specs=(vmem,) * 4,
         scratch_shapes=[
+            pltpu.VMEM(probe_fine.shape, jnp.int32),
+            pltpu.VMEM(probe_coarse.shape, jnp.int32),
+            pltpu.VMEM(kappa_fine.shape, F32),
+            pltpu.VMEM(kappa_coarse.shape, F32),
+            pltpu.VMEM(obs_weight.shape, F32),
+            pltpu.VMEM((1, blocks), jnp.int32),
             pltpu.VMEM(phi_tiles.shape, F32),
             pltpu.VMEM((blocks, 2 * tile, tile), BF16),
             field,
@@ -515,6 +556,7 @@
             pltpu.VMEM((4, 2, probes, rows + half_rows, tile), F32),
             pltpu.VMEM((2, 16, tile), F32),
             pltpu.VMEM((2, total, 16, tile), F32),
+            dma((6,)),
             dma((CHUNKS,)),
             dma((5, 2)),
             dma((5, 2)),
@@ -524,7 +566,7 @@
             dma((2, total)),
         ],
         compiler_params=pltpu.CompilerParams(
-            collective_id=0, has_side_effects=True, vmem_limit_bytes=40 * 2**20
+            collective_id=0, has_side_effects=True, vmem_limit_bytes=VMEM_BYTES
         ),
         cost_estimate=pl.CostEstimate(
             flops=4 * blocks * tile * tile * 8 * 4, bytes_accessed=phi_tiles.size * 4, transcendentals=0
@@ -539,6 +581,13 @@
         block_index.reshape(1, blocks),
         block_count,
     )
+    return pl.pallas_call(
+        write_out,
+        out_shape=tuple(jax.ShapeDtypeStruct(r.shape, F32) for r in results),
+        in_specs=[vmem] * 4,
+        out_specs=(pl.BlockSpec(memory_space=pltpu.HBM),) * 4,
+        scratch_shapes=[dma((4,))],
+    )(*results)
 
 
 def solution(mesh):

time: 45.4 us -> 35.2 us (0.78)
  local copies, waits for them, and re-layouts: 10.5 us -> 0 us
  Pallas kernels: 33.2 us -> 33.8 us
    unnamed x18 -> x0, local copies, waits for them, and re-layouts: 10.5 us -> none
    pallas_call x0 -> x1, Pallas kernels: none -> 1.74 us  [local(): pl.pallas_call(write_out, out_shape=tuple((jax.ShapeDtypeStruct(r.shape,...]
    pallas_call x1, Pallas kernels: 33.2 us -> 32 us  [local(): pl.pallas_call(functools.partial(kernel, n_ew, n_ns), out_shape=(jax.Shap...]
where the time goes in v2:
time: 35.2 us; the launch traced here: 35.1 us
  Pallas kernels  33.8 us (96%)
  between operations  1.29 us (4%)
    pallas_call x1, Pallas kernels, local(): pl.pallas_call(functools.partial(kernel, n_ew, n_ns), out_shape=(jax.Shap...  32 us
    pallas_call x1, Pallas kernels, local(): pl.pallas_call(write_out, out_shape=tuple((jax.ShapeDtypeStruct(r.shape,...  1.74 us

profile of v2, /device:TPU:0, one launch (start us, length us, event | category | flops | bytes accessed | tf_op | source)
XLA Modules:
  0.0 35.1 jit_solution(13438100009581987717)
XLA Ops:
  1.3 32.0 %shard_map.111 = (f32[4,32,256]{2,1,0:T(8,128)}, f32[4,16,128]{2,1,0:T(8,128)}, f32[4,32,256]{2,1,0:T(8,128)}, f32[4,16,128]{2,1,0:T(8,128)}) custom-call(s32[4,32,256]{2,1,0:T(8,128)} %pf_hbm.1, s32[4,16,128]{2,1,0:T(8,128)} %pc_hbm.1, f32[32,256]{1,0:T(8,128)} %kf_hbm.1, f32[16,128]{1,0:T(8,128)} %kc_hbm.1, f32[128,128,128]{2,1,0:T(8,128)} %phi_ref.1, ...), custom_call_target="tpu_custom_call" | custom-call | flops 268435456 | bytes 8388608 | tf_op jit(solution)/shard_map/pallas_call | solution.py:524
  33.3 1.7 %shard_map.112 = (f32[4,32,256]{2,1,0:T(8,128)}, f32[4,16,128]{2,1,0:T(8,128)}, f32[4,32,256]{2,1,0:T(8,128)}, f32[4,16,128]{2,1,0:T(8,128)}) custom-call(f32[4,32,256]{2,1,0:T(8,128)} %get-tuple-element.8.refs_0_, f32[4,16,128]{2,1,0:T(8,128)} %get-tuple-element.9.refs_1_, f32[4,32,256]{2,1,0:T(8,128)} %get-tuple-element.10.refs_2_, ...), custom_call_target="tpu_custom_call" | custom-call | tf_op jit(solution)/shard_map/pallas_call | solution.py:584

commit v3 on v2

--- a/solution.py
+++ b/solution.py
@@ -8,8 +8,7 @@
 from jax.sharding import PartitionSpec as P
 
 MESH = pl.DeviceIdType.MESH
-CHUNKS = 16
-GROUP = 16
+GROUP = 32
 VMEM_BYTES = 64 * 2**20 - 2**16
 F32 = jnp.float32
 BF16 = jnp.bfloat16
@@ -51,6 +50,7 @@
     pick,
     row_out,
     row_in,
+    col_out,
     col_in,
     ar_out,
     ar_in,
@@ -69,6 +69,7 @@
     blocks = ph.shape[0]
     at = (8, rows + 24, rows + half_rows + 40)
     size = (rows, half_rows, rows)
+    chunks = blocks // GROUP
     total = n_ew * n_ns
     e = lax.axis_index("ew")
     n = lax.axis_index("ns")
@@ -93,16 +94,15 @@
         input_copy(k).start()
 
     def phi_copy(c):
-        step = blocks // CHUNKS
-        return pltpu.make_async_copy(
-            phi_ref.at[pl.ds(c * step, step)], phi32.at[pl.ds(c * step, step)], phi_sem.at[c]
+        part = pl.ds(c * GROUP, GROUP)
+        return pltpu.make_async_copy(phi_ref.at[part], phi32.at[part], phi_sem.at[c]
         )
 
     def start_phi(c, _):
         phi_copy(c).start()
         return 0
 
-    lax.fori_loop(0, CHUNKS, start_phi, 0)
+    lax.fori_loop(0, chunks, start_phi, 0)
 
     def peer(k):
         other = lax.rem(me + k, total)
@@ -154,37 +154,44 @@
             def _():
                 row_copy(k, 1 - d).wait_recv()
 
-    def col_copies(field, k, d):
-        seg = 0 if d == 0 else 2
-        out = []
-        for j, (s, first) in enumerate(((seg, 0), (1, rows))):
-            out.append(
-                pltpu.make_async_remote_copy(
-                    src_ref=field.at[:, pl.ds(at[s], size[s]), :],
-                    dst_ref=col_in.at[k, 1 - d, :, pl.ds(first, size[s]), :],
-                    send_sem=col_ssem.at[k, d, j],
-                    recv_sem=col_rsem.at[k, 1 - d, j],
-                    device_id=col_dev[d],
-                    device_id_type=MESH,
-                )
-            )
-        return out
+    def turned(x, distance):
+        return pltpu.roll(x, distance % tile, 1) if distance % tile else x
+
+    def pack_cols(field, k):
+        for d in range(2):
+            edge = (0, tile - 1)[d]
+            for s, first in ((2 * d, 0), (1, rows)):
+                lane = lax.broadcasted_iota(jnp.int32, (size[s], tile), 1)
+                packed = jnp.zeros((size[s], tile), F32)
+                for p in range(probes):
+                    moved = turned(field[p, pl.ds(at[s], size[s]), :], p - edge)
+                    packed = jnp.where(lane == p, moved, packed)
+                col_out[k, d, pl.ds(first, size[s]), :] = packed
+
+    def col_copy(k, d):
+        return pltpu.make_async_remote_copy(
+            src_ref=col_out.at[k, d],
+            dst_ref=col_in.at[k, 1 - d],
+            send_sem=col_ssem.at[k, d],
+            recv_sem=col_rsem.at[k, 1 - d],
+            device_id=col_dev[d],
+            device_id_type=MESH,
+        )
 
     def col_start(field, k):
+        pack_cols(field, k)
         for d in range(2):
 
             @pl.when(has_col[d])
             def _():
-                for c in col_copies(field, k, d):
-                    c.start()
-
-    def col_wait(field, k):
+                col_copy(k, d).start()
+
+    def col_wait(k):
         for d in range(2):
 
             @pl.when(has_col[d])
             def _():
-                for c in col_copies(field, k, 1 - d):
-                    c.wait_recv()
+                col_copy(k, 1 - d).wait_recv()
 
     def pack_rows(field, k, first=0, outside=False):
         for s in range(3):
@@ -208,13 +215,11 @@
             return field[p, pl.ds(at[which], size[which]), :]
 
         first, last = (0, rows) if s != 1 else (rows, rows + half_rows)
-        low = seg(0) if s == 2 else col_in[k, 0, p, first:last, :]
-        high = seg(2) if s == 0 else col_in[k, 1, p, first:last, :]
+        low = turned(seg(0), 1) if s == 2 else turned(col_in[k, 0, first:last, :], -p)
+        high = turned(seg(2), -1) if s == 0 else turned(col_in[k, 1, first:last, :], -1 - p)
         centre = seg(s)
-        left = jnp.where(lane == 0, pltpu.roll(low, 1, 1), pltpu.roll(centre, 1, 1))
-        right = jnp.where(
-            lane == tile - 1, pltpu.roll(high, tile - 1, 1), pltpu.roll(centre, tile - 1, 1)
-        )
+        left = jnp.where(lane == 0, low, turned(centre, 1))
+        right = jnp.where(lane == tile - 1, high, turned(centre, -1))
         up = field[p, pl.ds(at[s] - 1, size[s]), :]
         down = field[p, pl.ds(at[s] + 1, size[s]), :]
         kap = kc_ref[...] if s == 1 else kf_ref[:, (s // 2) * tile : (s // 2 + 1) * tile]
@@ -262,16 +267,16 @@
     pick[...] = chosen.T.astype(BF16)
 
     def split_chunk(c, _):
-        step = blocks // CHUNKS
         phi_copy(c).wait()
-        for k in range(step):
-            x = phi32[c * step + k]
+        for k in range(GROUP):
+            x = phi32[c * GROUP + k]
             hi = x.astype(BF16)
-            ph[c * step + k, 0:tile, :] = hi
-            ph[c * step + k, tile : 2 * tile, :] = (x - hi.astype(F32)).astype(BF16)
+            ph[c * GROUP + k, 0:tile, :] = hi
+            ph[c * GROUP + k, tile : 2 * tile, :] = (x - hi.astype(F32)).astype(BF16)
         return 0
 
-    lax.fori_loop(0, CHUNKS, split_chunk, 0)
+    head = chunks // 2
+    lax.fori_loop(0, head, split_chunk, 0)
 
     def fill_ext(field):
         for p in range(probes):
@@ -310,8 +315,6 @@
             back[pl.ds(pl.multiple_of(b * 8, 8), 8), :] = out + pltpu.roll(out, 4, 0)
         return 0
 
-    steps = blocks // GROUP
-
     def scatter():
         for p in range(probes):
             x = back[pl.ds(p, blocks, stride=8), :]
@@ -358,7 +361,7 @@
 
     row_wait(0)
     unpack_rows(z, 0)
-    col_wait(z, 0)
+    col_wait(0)
     for p in range(probes):
         for s in range(3):
             put(u0, p, s, sar(z, 0, s, p))
@@ -366,11 +369,17 @@
     row_start(1)
     col_start(u0, 1)
     fill_ext(z)
-    lax.fori_loop(0, steps, observe, 0)
+
+    def observe_and_split(g, _):
+        observe(g, 0)
+        return split_chunk(g + head, 0)
+
+    lax.fori_loop(0, chunks - head, observe_and_split, 0)
+    lax.fori_loop(chunks - head, chunks, observe, 0)
     scatter()
     row_wait(1)
     unpack_rows(u0, 1)
-    col_wait(u0, 1)
+    col_wait(1)
     for p in range(probes):
         for s in range(3):
             put(q1, p, s, sar(u0, 1, s, p) + own(adj, p, s))
@@ -408,21 +417,21 @@
     ar_start(0)
 
     fill_ext(q1)
-    lax.fori_loop(0, steps // 2, observe, 0)
-    col_wait(q1, 2)
+    lax.fori_loop(0, head, observe, 0)
+    col_wait(2)
     for p in range(probes):
         for s in range(3):
             put(u1, p, s, sar(q1, 2, s, p))
     pack_rows(u1, 3)
     row_start(3)
     col_start(u1, 3)
-    lax.fori_loop(steps // 2, steps, observe, 0)
+    lax.fori_loop(head, chunks, observe, 0)
     scatter()
     pack_rows(adj, 4, outside=True)
     row_start(4)
     row_wait(3)
     unpack_rows(u1, 3)
-    col_wait(u1, 3)
+    col_wait(3)
     sums = ar_wait(0)
     rr, pq, qq = sums[0:4], sums[4:8], sums[8:12]
     alpha = rr / pq
@@ -478,13 +487,12 @@
             def _():
                 row_copy(k, d).wait_send()
 
-    for k, field in enumerate((z, u0, q1, u1)):
+    for k in range(4):
         for d in range(2):
 
             @pl.when(has_col[d])
             def _():
-                for c in col_copies(field, k, d):
-                    c.wait_send()
+                col_copy(k, d).wait_send()
 
     for k in range(2):
         for j in range(1, total):
@@ -553,15 +561,16 @@
             pltpu.VMEM((blocks, lines), BF16),
             pltpu.VMEM((5, 2, 3, 8, tile), F32),
             pltpu.VMEM((5, 2, 3, 8, tile), F32),
-            pltpu.VMEM((4, 2, probes, rows + half_rows, tile), F32),
+            pltpu.VMEM((4, 2, rows + half_rows, tile), F32),
+            pltpu.VMEM((4, 2, rows + half_rows, tile), F32),
             pltpu.VMEM((2, 16, tile), F32),
             pltpu.VMEM((2, total, 16, tile), F32),
             dma((6,)),
-            dma((CHUNKS,)),
+            dma((blocks // GROUP,)),
             dma((5, 2)),
             dma((5, 2)),
-            dma((4, 2, 2)),
-            dma((4, 2, 2)),
+            dma((4, 2)),
+            dma((4, 2)),
             dma((2, total)),
             dma((2, total)),
         ],

time: 35.2 us -> 31.9 us (0.906)
  Pallas kernels: 33.8 us -> 30.5 us
    pallas_call x1, Pallas kernels: 32 us -> 28.7 us  [local(): pl.pallas_call(functools.partial(kernel, n_ew, n_ns), out_shape=(jax.Shap...]
where the time goes in v3:
time: 31.9 us; the launch traced here: 31.8 us
  Pallas kernels  30.5 us (96%)
  between operations  1.29 us (4%)
    pallas_call x1, Pallas kernels, local(): pl.pallas_call(functools.partial(kernel, n_ew, n_ns), out_shape=(jax.Shap...  28.7 us
    pallas_call x1, Pallas kernels, local(): pl.pallas_call(write_out, out_shape=tuple((jax.ShapeDtypeStruct(r.shape,...  1.74 us

profile of v3, /device:TPU:0, one launch (start us, length us, event | category | flops | bytes accessed | tf_op | source)
XLA Modules:
  0.0 31.8 jit_solution(16071982648417569850)
XLA Ops:
  1.3 28.7 %shard_map.111 = (f32[4,32,256]{2,1,0:T(8,128)}, f32[4,16,128]{2,1,0:T(8,128)}, f32[4,32,256]{2,1,0:T(8,128)}, f32[4,16,128]{2,1,0:T(8,128)}) custom-call(s32[4,32,256]{2,1,0:T(8,128)} %pf_hbm.1, s32[4,16,128]{2,1,0:T(8,128)} %pc_hbm.1, f32[32,256]{1,0:T(8,128)} %kf_hbm.1, f32[16,128]{1,0:T(8,128)} %kc_hbm.1, f32[128,128,128]{2,1,0:T(8,128)} %phi_ref.1, ...), custom_call_target="tpu_custom_call" | custom-call | flops 268435456 | bytes 8388608 | tf_op jit(solution)/shard_map/pallas_call | solution.py:532
  30.0 1.7 %shard_map.112 = (f32[4,32,256]{2,1,0:T(8,128)}, f32[4,16,128]{2,1,0:T(8,128)}, f32[4,32,256]{2,1,0:T(8,128)}, f32[4,16,128]{2,1,0:T(8,128)}) custom-call(f32[4,32,256]{2,1,0:T(8,128)} %get-tuple-element.8.refs_0_, f32[4,16,128]{2,1,0:T(8,128)} %get-tuple-element.9.refs_1_, f32[4,32,256]{2,1,0:T(8,128)} %get-tuple-element.10.refs_2_, ...), custom_call_target="tpu_custom_call" | custom-call | tf_op jit(solution)/shard_map/pallas_call | solution.py:593

commit v4 on v3

--- a/solution.py
+++ b/solution.py
@@ -500,11 +500,15 @@
 
 
 def write_out(*refs):
-    sources, targets, sem = refs[:4], refs[4:8], refs[8]
-    copies = [pltpu.make_async_copy(sources[k], targets[k], sem.at[k]) for k in range(4)]
-    for copy in copies:
+    sources, targets, held, sem = refs[:4], refs[4:8], refs[8:12], refs[12]
+    reads = [pltpu.make_async_copy(sources[k], held[k], sem.at[0, k]) for k in range(4)]
+    writes = [pltpu.make_async_copy(held[k], targets[k], sem.at[1, k]) for k in range(4)]
+    for copy in reads:
         copy.start()
-    for copy in copies:
+    for k in range(4):
+        reads[k].wait()
+        writes[k].start()
+    for copy in writes:
         copy.wait()
 
 
@@ -593,9 +597,10 @@
     return pl.pallas_call(
         write_out,
         out_shape=tuple(jax.ShapeDtypeStruct(r.shape, F32) for r in results),
-        in_specs=[vmem] * 4,
+        in_specs=[pl.BlockSpec(memory_space=pltpu.HBM)] * 4,
         out_specs=(pl.BlockSpec(memory_space=pltpu.HBM),) * 4,
-        scratch_shapes=[dma((4,))],
+        scratch_shapes=[pltpu.VMEM(r.shape, F32) for r in results] + [dma((2, 4))],
+        compiler_params=pltpu.CompilerParams(vmem_limit_bytes=VMEM_BYTES),
     )(*results)
 
 

time: 31.9 us -> 31.9 us (level)
  no operation moved by 1% of the time
where the time goes in v4:
time: 31.9 us; the launch traced here: 31.8 us
  Pallas kernels  30.5 us (96%)
  between operations  1.29 us (4%)
    pallas_call x1, Pallas kernels, local(): pl.pallas_call(functools.partial(kernel, n_ew, n_ns), out_shape=(jax.Shap...  28.7 us
    pallas_call x1, Pallas kernels, local(): pl.pallas_call(write_out, out_shape=tuple((jax.ShapeDtypeStruct(r.shape,...  1.72 us

profile of v4, /device:TPU:0, one launch (start us, length us, event | category | flops | bytes accessed | tf_op | source)
XLA Modules:
  0.0 31.8 jit_solution(7856419929446998393)
XLA Ops:
  1.3 28.7 %shard_map.111 = (f32[4,32,256]{2,1,0:T(8,128)}, f32[4,16,128]{2,1,0:T(8,128)}, f32[4,32,256]{2,1,0:T(8,128)}, f32[4,16,128]{2,1,0:T(8,128)}) custom-call(s32[4,32,256]{2,1,0:T(8,128)} %pf_hbm.1, s32[4,16,128]{2,1,0:T(8,128)} %pc_hbm.1, f32[32,256]{1,0:T(8,128)} %kf_hbm.1, f32[16,128]{1,0:T(8,128)} %kc_hbm.1, f32[128,128,128]{2,1,0:T(8,128)} %phi_ref.1, ...), custom_call_target="tpu_custom_call" | custom-call | flops 268435456 | bytes 8388608 | tf_op jit(solution)/shard_map/pallas_call | solution.py:536
  30.0 1.7 %shard_map.112 = (f32[4,32,256]{2,1,0:T(8,128)}, f32[4,16,128]{2,1,0:T(8,128)}, f32[4,32,256]{2,1,0:T(8,128)}, f32[4,16,128]{2,1,0:T(8,128)}) custom-call(f32[4,32,256]{2,1,0:T(8,128)} %get-tuple-element.8.refs_0_, f32[4,16,128]{2,1,0:T(8,128)} %get-tuple-element.9.refs_1_, f32[4,32,256]{2,1,0:T(8,128)} %get-tuple-element.10.refs_2_, ...), custom_call_target="tpu_custom_call" | custom-call | tf_op jit(solution)/shard_map/pallas_call | solution.py:597
